TPU v7x, 128 devices: a whole 4x4x4 slice. The times are simulated.
128 devices in a mesh: row: 8 (over z, core), col: 16 (over x, y).
Axes of the slice: x: 4, y: 4, z: 4, core: 2. Of those that a mesh axis runs over, the one named last changes fastest.
Arguments:
- features: bfloat16 [256, 512, 256], P('row', 'col'), may hold values from -6 to 6
- conv_weight: bfloat16 [3, 3, 256, 256], replicated, may hold values from -0.125 to 0.125
- first_weight: bfloat16 [12544, 1024], P(('row', 'col')), may hold values from -0.0546875 to 0.0546875
- second_weight: bfloat16 [1024, 1024], replicated, may hold values from -0.1875 to 0.1875
- out_weight: bfloat16 [1024, 42], replicated, may hold values from -0.1875 to 0.1875
- roi_count: int32 [128], P(('row', 'col')), may hold values from 32 to 256, as said below
- roi_row: int32 [32768], P(('row', 'col')), may hold values from 4 to 27
- roi_col: int32 [32768], P(('row', 'col')), may hold values from 4 to 27
- roi_angle: int32 [32768], P(('row', 'col')), may hold values from 0 to 7
- roi_label: int32 [32768], P(('row', 'col')), may hold values from 0 to 37
- roi_target: bfloat16 [32768, 5], P(('row', 'col')), may hold values from -4 to 4
Outputs:
- neck: bfloat16 [256, 512, 256], P('row', 'col')
- feat_grad: float32 [256, 512, 256], P('row', 'col')
- second_grad: float32 [1024, 1024], replicated
- out_grad: float32 [1024, 42], replicated
Inputs may be any that keep to these rules, and one draw needn't show every extreme that they name: `roi_count`: A tile's live RoIs fill its first slots; in every draw some tile has all 256 slots live.
All inputs are finite; a program needn't handle non-finite values.
Results may differ from a plain program's by a relative error of at most 0.01.
Values may be sent and summed in bfloat16 or wider, within the bound.
A program may use at most 192 MiB of HBM per device.

v0:
```python
import math

import jax
import jax.numpy as jnp
import numpy as np
from jax import lax
from jax.sharding import PartitionSpec as P

POOL = 7
ANGLES = 8


prior_logit = -4.59512


def extended(value, sides, width):
    for axis, dim in sides:
        size, length = (lax.axis_size(axis), value.shape[dim])
        up = [(i, (i + 1) % size) for i in range(size - 1)]
        down = [(j, i) for i, j in up]
        last = lax.slice_in_dim(value, length - width, length, axis=dim)
        initial = lax.slice_in_dim(value, 0, width, axis=dim)
        before = lax.ppermute(last, axis, up)
        after = lax.ppermute(initial, axis, down)
        value = jnp.concatenate([before, value, after], axis=dim)
    return value


def offset_tables(pool, angles):
    turn = np.arange(angles) * math.pi / angles
    along = np.arange(pool) - pool // 2
    down = (along[:, None] * np.ones((1, pool))).reshape(1, -1)
    across = (np.ones((pool, 1)) * along[None, :]).reshape(1, -1)
    cosine = np.cos(turn)[:, None]
    sine = np.sin(turn)[:, None]
    shift_rows = np.floor(down * cosine - across * sine + 0.5).astype(np.int32)
    shift_cols = np.floor(down * sine + across * cosine + 0.5).astype(np.int32)
    return (shift_rows, shift_cols)


def sample_cells(centre_row, centre_col, angle, width):
    shift_rows, shift_cols = offset_tables(POOL, ANGLES)
    choose = (angle[:, None] == jnp.arange(ANGLES, dtype=jnp.int32)[None, :]).astype(jnp.int32)
    drow = jnp.sum(choose[:, :, None] * jnp.asarray(shift_rows)[None], axis=1)
    dcol = jnp.sum(choose[:, :, None] * jnp.asarray(shift_cols)[None], axis=1)
    return ((centre_row[:, None] + drow) * width + centre_col[:, None] + dcol).astype(jnp.int32)


def slope(value):
    return 0.5 * (1.0 + jax.scipy.special.erf(value / math.sqrt(2.0))) + value * jnp.exp(
        -0.5 * value * value
    ) / math.sqrt(2.0 * math.pi)


def block_rows(count):
    step_rows = 128
    while count % step_rows != 0:
        step_rows = step_rows // 2
    return step_rows


def head_block(blocks, labels, targets, live, first_w, second_w, out_w):
    classes = out_w.shape[1] - targets.shape[1]
    pre1 = jnp.dot(blocks, first_w, preferred_element_type=jnp.float32)
    hid1 = jax.nn.gelu(pre1, approximate=False).astype(jnp.bfloat16)
    pre2 = jnp.dot(hid1, second_w, preferred_element_type=jnp.float32)
    hid2 = jax.nn.gelu(pre2, approximate=False).astype(jnp.bfloat16)
    z = jnp.dot(hid2, out_w, preferred_element_type=jnp.float32)
    onehot = (labels[:, None] == jnp.arange(classes, dtype=jnp.int32)[None, :]).astype(jnp.float32)
    foreground = (labels < classes).astype(jnp.float32)[:, None]
    dlogit = jax.nn.sigmoid(z[:, :classes] + prior_logit) - onehot
    dbox = jnp.clip(z[:, classes:] - targets.astype(jnp.float32), -1.0, 1.0) * foreground
    dz = jnp.where(live[:, None], jnp.concatenate([dlogit, dbox], axis=1), 0.0).astype(jnp.bfloat16)
    contract_rows = (((0,), (0,)), ((), ()))
    contract_cols = (((1,), (1,)), ((), ()))
    out_grad = lax.dot_general(hid2, dz, contract_rows, preferred_element_type=jnp.float32)
    dpre2 = (
        lax.dot_general(dz, out_w, contract_cols, preferred_element_type=jnp.float32) * slope(pre2)
    ).astype(jnp.bfloat16)
    second_grad = lax.dot_general(hid1, dpre2, contract_rows, preferred_element_type=jnp.float32)
    dpre1 = (
        lax.dot_general(dpre2, second_w, contract_cols, preferred_element_type=jnp.float32)
        * slope(pre1)
    ).astype(jnp.bfloat16)
    dblocks = lax.dot_general(
        dpre1, first_w, contract_cols, preferred_element_type=jnp.float32
    ).astype(jnp.bfloat16)
    return (dblocks, second_grad, out_grad)


def run_blocks(work, labels, targets, live, active, first_w, second_w, out_w):
    nrows = work.shape[0]
    step_rows = block_rows(nrows)
    block_count = (active + step_rows - 1) // step_rows

    def advance(index, carry):
        dwork, second_sum, out_sum = carry
        start = (index * step_rows).astype(jnp.int32)
        rows = lax.dynamic_slice_in_dim(work, start, step_rows, 0)
        label_rows = lax.dynamic_slice_in_dim(labels, start, step_rows, 0)
        target_rows = lax.dynamic_slice_in_dim(targets, start, step_rows, 0)
        live_rows = lax.dynamic_slice_in_dim(live, start, step_rows, 0)
        drows, second_part, out_part = head_block(
            rows, label_rows, target_rows, live_rows, first_w, second_w, out_w
        )
        dwork = lax.dynamic_update_slice_in_dim(dwork, drows, start, 0)
        return (dwork, second_sum + second_part, out_sum + out_part)

    init = (
        jnp.zeros_like(work),
        jnp.zeros((second_w.shape[0], second_w.shape[1]), jnp.float32),
        jnp.zeros((out_w.shape[0], out_w.shape[1]), jnp.float32),
    )
    return lax.fori_loop(0, block_count, advance, init)


def sample_blocks(neck_flat, cells):
    cell_total, channels = neck_flat.shape
    slots = cells.shape[0]
    step_rows = block_rows(slots)
    grouped = cells.reshape(slots // step_rows, step_rows * POOL * POOL)

    def pick(indices):
        onehot = (indices[:, None] == jnp.arange(cell_total, dtype=jnp.int32)[None, :]).astype(
            jnp.bfloat16
        )
        return jnp.dot(onehot, neck_flat, preferred_element_type=jnp.float32).astype(jnp.bfloat16)

    picked = lax.map(pick, grouped)
    return picked.reshape(slots, POOL * POOL * channels)


def spread_grads(dblocks, cells, cell_total, channels):
    slots = cells.shape[0]
    step_rows = block_rows(slots)
    grouped_cells = cells.reshape(slots // step_rows, step_rows * POOL * POOL)
    grouped_grads = dblocks.reshape(slots // step_rows, step_rows * POOL * POOL, channels)

    def add_group(total, pair):
        indices, rows = pair
        onehot = (indices[:, None] == jnp.arange(cell_total, dtype=jnp.int32)[None, :]).astype(
            jnp.bfloat16
        )
        part = lax.dot_general(
            onehot, rows, (((0,), (0,)), ((), ())), preferred_element_type=jnp.float32
        )
        return (total + part, None)

    total, unused = lax.scan(
        add_group, jnp.zeros((cell_total, channels), jnp.float32), (grouped_cells, grouped_grads)
    )
    return total


def on_device(
    features,
    conv_weight,
    first_weight,
    second_weight,
    out_weight,
    roi_count,
    roi_row,
    roi_col,
    roi_angle,
    roi_label,
    roi_target,
):
    tile_h, tile_w, channels = features.shape
    padded = extended(features, (("row", 0), ("col", 1)), 1)
    total_conv = jnp.zeros((tile_h * tile_w, conv_weight.shape[3]), jnp.float32)
    for first in range(3):
        for second in range(3):
            window = padded[first : first + tile_h, second : second + tile_w, :].reshape(
                tile_h * tile_w, channels
            )
            total_conv = total_conv + jnp.dot(
                window, conv_weight[first, second], preferred_element_type=jnp.float32
            )
    neck_flat = total_conv.astype(jnp.bfloat16)
    first_full = lax.all_gather(first_weight, ("row", "col"), axis=0, tiled=True)
    slots = roi_row.shape[0]
    cells = sample_cells(roi_row, roi_col, roi_angle, tile_w)
    blocks = sample_blocks(neck_flat, cells)
    count = roi_count[0]
    position = jnp.arange(slots, dtype=jnp.int32)
    dblocks, second_sum, out_sum = run_blocks(
        blocks,
        roi_label,
        roi_target,
        position < count,
        count,
        first_full,
        second_weight,
        out_weight,
    )
    feat_grad = spread_grads(dblocks, cells, tile_h * tile_w, channels)
    second_grad, out_grad = lax.psum((second_sum, out_sum), ("row", "col"))
    return (
        neck_flat.reshape(tile_h, tile_w, channels),
        feat_grad.reshape(tile_h, tile_w, channels),
        second_grad,
        out_grad,
    )


def solution(mesh):
    in_specs = (
        P("row", "col", None),
        P(),
        P(("row", "col"), None),
        P(),
        P(),
        P(("row", "col")),
        P(("row", "col")),
        P(("row", "col")),
        P(("row", "col")),
        P(("row", "col")),
        P(("row", "col"), None),
    )
    out_specs = (P("row", "col", None), P("row", "col", None), P(), P())
    return jax.shard_map(
        on_device, mesh=mesh, in_specs=in_specs, out_specs=out_specs, check_vma=False
    )
```

profile of v0, /device:TPU:1, one launch (start us, length us, event | category | flops | bytes accessed | tf_op | source)
XLA Modules:
  0.0 390.8 jit_solution(16586853725560954634)
XLA Ops:
  7.2 0.0 all-gather.3.cloned.1.call-start
  7.2 0.7 all-gather.3.cloned.1.call-update
  7.9 0.0 all-reduce.3.cloned.1.call-start
  8.0 0.7 fusion.109
  8.7 3.3 collective-permute-start.1
  12.0 3.5 collective-permute-start
  16.2 0.7 fusion.107
  16.9 1.1 multiply_reduce_fusion.1
  18.0 0.1 copy.17
  18.1 0.2 reduce_sum.23
  18.3 0.1 copy.18
  18.4 0.2 reduce_sum.25
  18.6 0.8 add.115
  19.4 0.2 add.116
  19.6 0.8 add.119
  20.4 0.2 add.120
  20.6 0.1 add_add_fusion
  20.8 1.6 pad_maximum_fusion.3
  22.4 0.1 fusion.108
  22.4 3.2 collective-permute-start.2
  25.7 1.3 collective-permute-start.3
  27.0 0.3 fusion.88
  27.3 0.3 fusion.95
  27.6 2.8 collective-permute-done.3
  30.4 0.9 pad_maximum_fusion.2
  31.3 0.3 fusion.86
  31.6 0.3 convolution_add_fusion.7
  31.9 0.3 convolution_add_fusion.6
  32.2 0.3 convolution_add_fusion.5
  32.5 0.1 copy-done.3
  32.6 0.3 convolution_add_fusion.4
  32.9 0.3 convolution_add_fusion.3
  33.2 0.3 fusion.81
  33.6 13.3 %while.35 = (s32[]{:T(128)}, bf16[2,6272,256]{2,1,0:T(8,128)(2,1)}, s32[2,6272]{1,0:T(2,128)S(1)}, bf16[1024,256]{1,0:T(8,128)(2,1)S(1)}, s32[]{:T(128)}) while((s32[]{:T(128)}, bf16[2,6272,256]{2,1,0:T(8,128)(2,1)}, s32[2,6272]{1,0:T(2,128)S(1)}, bf16[1024,256]{1,0:T(8,128)(2,1)S(1)}, s32[]{:T(128)}) %tuple.70), condition=%wide.region_3.4_spmd, body=%wide.region_2.3_spmd.sunk | while | flops 3296362496 | bytes 3810893 | solution.py:129
  33.6 0.1 dynamic-slice_reduce_fusion.4
  33.7 6.6 %fusion.157 = bf16[2,6272,256]{2,1,0:T(8,128)(2,1)} fusion(bf16[2,6272,256]{2,1,0:T(8,128)(2,1)} %get-tuple-element.335, s32[]{:T(128)S(6)} %copy.25, bf16[1024,256]{1,0:T(8,128)(2,1)S(1)} %get-tuple-element.342, s32[6272]{0:T(1024)S(1)} %dynamic-slice_reduce_fusion.4), kind=kOutput, calls=%fused_computation.96.clone.1 | convolution fusion | flops 3296362496 | bytes 3760644 | tf_op jit(solution)/shard_map/while/body/eval_jaxpr/dot_general | solution.py:127
  40.2 0.1 dynamic-slice_reduce_fusion.4
  40.3 6.6 %fusion.157 = bf16[2,6272,256]{2,1,0:T(8,128)(2,1)} fusion(bf16[2,6272,256]{2,1,0:T(8,128)(2,1)} %get-tuple-element.335, s32[]{:T(128)S(6)} %copy.25, bf16[1024,256]{1,0:T(8,128)(2,1)S(1)} %get-tuple-element.342, s32[6272]{0:T(1024)S(1)} %dynamic-slice_reduce_fusion.4), kind=kOutput, calls=%fused_computation.96.clone.1 | convolution fusion | flops 3296362496 | bytes 3760644 | tf_op jit(solution)/shard_map/while/body/eval_jaxpr/dot_general | solution.py:127
  46.9 12.4 %reshape.100 = bf16[256,12544]{1,0:T(8,128)(2,1)} reshape(bf16[2,6272,256]{2,1,0:T(8,128)(2,1)} %get-tuple-element.113) | data formatting | bytes 12845056 | tf_op jit(solution)/shard_map/reshape | solution.py:130
  59.3 53.3 %all-gather.3.cloned.1.call-done = bf16[128,98,1024]{2,1,0:T(8,128)(2,1)} async-done(((bf16[1,98,1024]{2,1,0:T(8,128)(2,1)}), bf16[128,98,1024]{2,1,0:T(8,128)(2,1)}) %all-gather.3.cloned.1.call-update) | async-done | bytes 25690128 | tf_op jit(solution)/shard_map/all_gather | solution.py:180
  112.6 32.4 %reshape.104 = bf16[12544,1024]{1,0:T(8,128)(2,1)} reshape(bf16[128,98,1024]{2,1,0:T(8,128)(2,1)} %all-gather.3.cloned.1.call-done) | data formatting | bytes 51380224
  145.0 2.5 broadcast_in_dim.26
  147.6 3.1 broadcast_in_dim.25
  150.7 36.5 %while.36 = (s32[]{:T(128)}, bf16[256,12544]{1,0:T(8,128)(2,1)}, f32[1024,1024]{1,0:T(8,128)}, f32[1024,42]{0,1:T(8,128)S(1)}, s32[]{:T(128)}, /*index=5*/pred[2...) while((s32[]{:T(128)}, bf16[256,12544]{1,0:T(8,128)(2,1)}, ...), condition=%wide.region_5.6_spmd, body=%wide.region_4.5_spmd.sunk | while | flops 7445978112 | bytes 75700184 | solution.py:114
  150.9 0.1 dynamic_slice.48
  150.9 0.1 compare_convert_fusion.2
  151.0 11.1 %fusion.172 = f32[128,1024]{1,0:T(8,128)S(1)} fusion(bf16[12544,1024]{1,0:T(8,128)(2,1)} %get-tuple-element.383, bf16[256,12544]{1,0:T(8,128)(2,1)} %get-tuple-element.382, s32[]{:T(128)S(6)} %select_n.27), kind=kOutput, calls=%fused_computation.2.clone.1 | convolution fusion | flops 3288334336 | bytes 29425668 | tf_op jit(solution)/shard_map/while/body/dot_general | solution.py:64
  162.1 2.4 fusion.173
  164.5 0.2 fusion.174
  164.7 0.3 fusion.177
  165.1 0.2 convolution_add_fusion.11
  165.3 6.0 %convolution_add_fusion.10 = f32[1024,1024]{1,0:T(8,128)} fusion(f32[1024,1024]{1,0:T(8,128)} %get-tuple-element.362, bf16[128,1024]{1,0:T(8,128)(2,1)S(1)} %fusion.177, f32[128,1024]{1,0:T(8,128)S(1)} %fusion.172), kind=kOutput, calls=%fused_computation.4.clone.1 | convolution fusion | flops 278003712 | bytes 9175040 | tf_op jit(solution)/shard_map/while/body/dot_general | solution.py:80
  171.2 15.9 %fusion.178 = bf16[256,12544]{1,0:T(8,128)(2,1)} fusion(bf16[256,12544]{1,0:T(8,128)(2,1)} %get-tuple-element.361, s32[]{:T(128)S(6)} %select_n.27, bf16[12544,1024]{1,0:T(8,128)(2,1)} %get-tuple-element.383, bf16[128,1024]{1,0:T(8,128)(2,1)S(1)} %fusion.177, bf16[1024,1024]{1,0:T(8,128)(2,1)S(1)} %get-tuple-element.384, f32[128,1024]{1,0:T(8,128)S(1)} %fusion.172), kind=kOutput, calls=%fused_computation.1.clone.1 | convolution fusion | flops 3559686144 | bytes 31784964 | tf_op jit(solution)/shard_map/while/body/dot_general | solution.py:85
  187.2 0.7 copy-done.1
  187.9 0.0 all-reduce.3.cloned.1.call-update
  187.9 13.8 %reshape.101 = bf16[2,6272,256]{2,1,0:T(8,128)(2,1)} reshape(bf16[256,12544]{1,0:T(8,128)(2,1)} %get-tuple-element.114) | data formatting | bytes 12845056 | tf_op jit(solution)/shard_map/reshape | solution.py:137
  201.7 20.3 %while.37 = (s32[]{:T(128)}, f32[1024,256]{1,0:T(8,128)S(1)}, s32[2,6272]{1,0:T(2,128)S(1)}, bf16[2,6272,256]{2,1,0:T(8,128)(2,1)}, s32[]{:T(128)}, /*index=5*/s32[]{:T(128)}) while((s32[]{:T(128)}, f32[1024,256]{1,0:T(8,128)S(1)}, s32[2,6272]{1,0:T(2,128)S(1)}, bf16[2,6272,256]{2,1,0:T(8,128)(2,1)}, s32[]{:T(128)}, ...), condition=%wide.region_7.8_spmd.clone, body=%wide.region_6.7_spmd.clone.sunk | while | flops 3295281152 | bytes 5383775 | solution.py:149
  201.7 0.1 dynamic-slice_reduce_fusion.5
  201.8 10.0 %fusion.180 = f32[1024,256]{1,0:T(8,128)S(1)} fusion(bf16[2,6272,256]{2,1,0:T(8,128)(2,1)} %get-tuple-element.407, s32[]{:T(128)S(6)} %copy.43, s32[6272]{0:T(1024)S(1)} %dynamic-slice_reduce_fusion.5, f32[1024,256]{1,0:T(8,128)S(1)} %get-tuple-element.399, pred[]{:T(512)S(6)} %compare.5), kind=kOutput, calls=%fused_computation.103.clone.1 | convolution fusion | flops 3295281152 | bytes 5333509 | tf_op jit(solution)/shard_map/while/body/eval_jaxpr/dot_general | solution.py:144
  211.8 0.1 dynamic-slice_reduce_fusion.5
  211.9 10.0 %fusion.180 = f32[1024,256]{1,0:T(8,128)S(1)} fusion(bf16[2,6272,256]{2,1,0:T(8,128)(2,1)} %get-tuple-element.407, s32[]{:T(128)S(6)} %copy.43, s32[6272]{0:T(1024)S(1)} %dynamic-slice_reduce_fusion.5, f32[1024,256]{1,0:T(8,128)S(1)} %get-tuple-element.399, pred[]{:T(512)S(6)} %compare.5), kind=kOutput, calls=%fused_computation.103.clone.1 | convolution fusion | flops 3295281152 | bytes 5333509 | tf_op jit(solution)/shard_map/while/body/eval_jaxpr/dot_general | solution.py:144
  222.0 156.5 %all-reduce.3.cloned.1.call-done = (f32[1024,1024]{1,0:T(8,128)}, f32[1024,42]{0,1:T(8,128)}) async-done(((f32[1024,1024]{1,0:T(8,128)}, f32[1024,42]{0,1:T(8,128)}), (f32[1024,1024]{1,0:T(8,128)}, f32[1024,42]{0,1:T(8,128)})) %all-reduce.3.cloned.1.call-update) | async-done | bytes 4366352 | tf_op jit(solution)/shard_map/psum | solution.py:197
  378.5 4.8 %copy.50 = f32[1024,1024]{1,0:T(8,128)} copy(f32[1024,1024]{1,0:T(8,128)} %get-tuple-element.412) | data formatting | bytes 8388608
  383.3 0.7 copy.51
  (33 shorter events, 0.1 us)
Async XLA Ops:
  7.2 19.8 %copy-start.6 = (bf16[3,3,256,256]{3,2,1,0:T(8,128)(2,1)S(1)}, bf16[3,3,256,256]{3,2,1,0:T(8,128)(2,1)}, u32[]{:S(2)}) copy-start(bf16[3,3,256,256]{3,2,1,0:T(8,128)(2,1)} %param.20) | copy-start | bytes 3538948
  7.2 105.4 %all-gather.3.cloned.1.call-start = ((), (), s32[]{:S(2)}) async-start(), calls=%async_computation | async-start | bytes 27475968 | tf_op jit(solution)/shard_map/all_gather | solution.py:180
  7.9 370.6 %all-reduce.3.cloned.1.call-start = ((), (), s32[]{:S(2)}) async-start(), calls=%async_computation.1 | async-start | bytes 8781824 | tf_op jit(solution)/shard_map/psum | solution.py:197
  8.7 12.1 %collective-permute-start.1 = (bf16[1,32,256]{2,1,0:T(8,128)(2,1)S(1)}, bf16[1,32,256]{2,1,0:T(8,128)(2,1)S(1)}, u32[]{:S(2)}, u32[]{:S(2)}) collective-permute-start(bf16[1,32,256]{2,1,0:T(8,128)(2,1)S(1)} %get-tuple-element.195), channel_id=1, source_target_pairs={{16,0},{32,16},{48,32},{64,48},{80,64},{96,80},{112,96},{17,1},{33... | collective-permute-start | bytes 49160 | tf_op jit(solution)/shard_map/ppermute | solution.py:24
  12.0 8.7 %collective-permute-start = (bf16[1,32,256]{2,1,0:T(8,128)(2,1)S(1)}, bf16[1,32,256]{2,1,0:T(8,128)(2,1)S(1)}, u32[]{:S(2)}, u32[]{:S(2)}) collective-permute-start(bf16[1,32,256]{2,1,0:T(8,128)(2,1)S(1)} %get-tuple-element.196), channel_id=1, source_target_pairs={{0,16},{16,32},{32,48},{48,64},{64,80},{80,96},{96,112},{1,17},{17... | collective-permute-start | bytes 49160 | tf_op jit(solution)/shard_map/ppermute | solution.py:23
  22.4 5.1 %collective-permute-start.2 = (bf16[34,1,256]{2,1,0:T(2,128)(2,1)S(1)}, bf16[34,1,256]{2,1,0:T(2,128)(2,1)S(1)}, u32[]{:S(2)}, u32[]{:S(2)}) collective-permute-start(bf16[34,1,256]{2,1,0:T(2,128)(2,1)S(1)} %get-tuple-element.190), channel_id=1, source_target_pairs={{0,1},{1,2},{2,3},{3,4},{4,5},{5,6},{6,7},{7,8},{8,9},{9,10},{10,1... | collective-permute-start | bytes 52232 | tf_op jit(solution)/shard_map/ppermute | solution.py:23
  25.7 4.8 %collective-permute-start.3 = (bf16[34,1,256]{2,1,0:T(2,128)(2,1)S(1)}, bf16[34,1,256]{2,1,0:T(2,128)(2,1)S(1)}, u32[]{:S(2)}, u32[]{:S(2)}) collective-permute-start(bf16[34,1,256]{2,1,0:T(2,128)(2,1)S(1)} %get-tuple-element.191), channel_id=1, source_target_pairs={{1,0},{2,1},{3,2},{4,3},{5,4},{6,5},{7,6},{8,7},{9,8},{10,9},{11,1... | collective-permute-start | bytes 52232 | tf_op jit(solution)/shard_map/ppermute | solution.py:24
  31.6 1.0 copy-start.3
  46.9 12.4 %copy-start.4 = (s32[2,6272]{1,0:T(2,128)}, s32[2,6272]{1,0:T(2,128)S(1)}, u32[]{:S(2)}) copy-start(s32[2,6272]{1,0:T(2,128)S(1)} %get-tuple-element.424) | copy-start | bytes 150532
  46.9 12.4 %copy-start.7 = (bf16[1024,256]{1,0:T(8,128)(2,1)}, bf16[1024,256]{1,0:T(8,128)(2,1)S(1)}, u32[]{:S(2)}) copy-start(bf16[1024,256]{1,0:T(8,128)(2,1)S(1)} %get-tuple-element.425) | copy-start | bytes 1572868
  147.5 3.1 copy-start
  147.5 3.1 copy-start.2
  147.5 3.1 copy-start.9
  147.5 3.1 copy-start.10
  187.2 0.7 copy-start.1
  187.9 13.8 %copy-start.5 = (s32[2,6272]{1,0:T(2,128)S(1)}, s32[2,6272]{1,0:T(2,128)}, u32[]{:S(2)}) copy-start(s32[2,6272]{1,0:T(2,128)} %copy-done.4) | copy-start | bytes 150532
  222.0 161.3 %copy-start.11 = (f32[1024,256]{1,0:T(8,128)}, f32[1024,256]{1,0:T(8,128)S(1)}, u32[]{:S(2)}) copy-start(f32[1024,256]{1,0:T(8,128)S(1)} %get-tuple-element.115) | copy-start | bytes 3145732
  378.5 4.8 %copy-start.8 = (f32[1024,42]{0,1:T(8,128)S(1)}, f32[1024,42]{0,1:T(8,128)}, u32[]{:S(2)}) copy-start(f32[1024,42]{0,1:T(8,128)} %get-tuple-element.413) | copy-start | bytes 516100
Sparse Core Ops, SparseCore 0:
  11.0 101.5 all-gather.2
  188.0 190.4 all-reduce.2
where the time goes:
time: 393 us; the launch traced here: 391 us
  waiting for transfers between devices  213 us (54%)
  local copies, waits for them, and re-layouts  74.5 us (19%)
  matrix products  72 us (18%)
  between operations  15 us (4%)
  starting transfers between devices  11.4 us (3%)
  other arithmetic  4.36 us (1%)
    psum x1, waiting for transfers between devices, on_device(): second_grad, out_grad = lax.psum((second_sum, out_sum), ('row', 'col'))  157 us
    all_gather x1, waiting for transfers between devices, on_device(): lax.all_gather(first_weight, ('row', 'col'), axis=0, tiled=True)  53.3 us
    unnamed x28, local copies, waits for them, and re-layouts  38.8 us
    dot_general x2, matrix products, add_group(): lax.dot_general(onehot, rows, (((0,), (0,)), ((), ())), preferred_element...  20.1 us
    dot_general x1, matrix products, head_block(): lax.dot_general(dpre1, first_w, contract_cols, preferred_element_type=jnp...  15.9 us
    reshape x1, local copies, waits for them, and re-layouts, spread_grads(): dblocks.reshape(slots // step_rows, step_rows * POOL * POOL, channels)  13.8 us
    dot_general x2, matrix products, pick(): jnp.dot(onehot, neck_flat, preferred_element_type=jnp.float32)  13.1 us
    reshape x1, local copies, waits for them, and re-layouts, sample_blocks(): return picked.reshape(slots, POOL * POOL * channels)  12.4 us
  transfers between devices with their start and end apart: 6, of which 3 were waited for; matrix products, arithmetic and copies ran while one was open for 18% of the time, Pallas kernels for 0%

commit v1 on v0

v1 whole, which is shorter than its diff:
```python
import functools
import math

import jax
import jax.numpy as jnp
import numpy as np
from jax import lax
from jax.experimental import pallas as pl
from jax.experimental.pallas import tpu as pltpu
from jax.sharding import PartitionSpec as P

POOL = 7
ANGLES = 8
CLASSES = 37
OUTS = 42
HID = 1024
CH = 256
CELLS = 1024
ROIS = 256
SAMPLES = POOL * POOL
GROUP = 784
SPAN = POOL * CH
WIDE = HID + 128
COLS = WIDE // 3
MESH = pl.DeviceIdType.MESH

prior_logit = -4.59512

PARTS = (
    (0, 128, 256, "xyz"),
    (256, 128, 256, "yzx"),
    (512, 144, 272, "zxy"),
)


def offset_tables(pool, angles):
    turn = np.arange(angles) * math.pi / angles
    along = np.arange(pool) - pool // 2
    down = (along[:, None] * np.ones((1, pool))).reshape(1, -1)
    across = (np.ones((pool, 1)) * along[None, :]).reshape(1, -1)
    cosine = np.cos(turn)[:, None]
    sine = np.sin(turn)[:, None]
    shift_rows = np.floor(down * cosine - across * sine + 0.5).astype(np.int32)
    shift_cols = np.floor(down * sine + across * cosine + 0.5).astype(np.int32)
    return (shift_rows, shift_cols)


def erf_parts(value):
    return 0.5 * (1.0 + lax.erf(value * math.sqrt(0.5)))


def slope(value, phi):
    return phi + value * jnp.exp(-0.5 * value * value) * (1.0 / math.sqrt(2.0 * math.pi))


def dot(a, b):
    return jnp.dot(a, b, preferred_element_type=jnp.float32)


def dot_nt(a, b):
    return lax.dot_general(a, b, (((1,), (1,)), ((), ())), preferred_element_type=jnp.float32)


def dot_tn(a, b):
    return lax.dot_general(a, b, (((0,), (0,)), ((), ())), preferred_element_type=jnp.float32)


def kernel(
    feat,
    edge_cols,
    conv_w,
    shard,
    w2,
    wo,
    meta,
    meta_t,
    table,
    table_t,
    neck,
    feat_grad,
    total,
    wf,
    stage,
    slots,
    halo_row,
    halo_col,
    halo_corner,
    side,
    ext,
    taps,
    x,
    cells_t,
    pre1,
    gp1,
    pre2,
    gp2,
    hid1,
    dpre2,
    dpre1,
    dxs,
    keep,
    send0,
    recv0,
    send1,
    recv1,
    keep1,
    send2,
    recv2,
    keep2,
    recv3,
    halo_s,
    halo_r,
    group_s,
    group_r,
    ring_s,
    ring_r,
    sib_s,
    sib_r,
    red_s,
    red_r,
):
    row = lax.axis_index("row")
    col = lax.axis_index("col")
    pos = {"x": col // 4, "y": lax.rem(col, 4), "z": row // 2}
    core = lax.rem(row, 2)

    def device(axis, step):
        at = dict(pos)
        at[axis] = lax.rem(pos[axis] + (step + 4), 4)
        return (at["z"] * 2 + core, at["x"] * 4 + at["y"])

    sibling = (row + 1 - 2 * core, col)
    member = lax.rem(col, 8)

    def group_device(step):
        return (row, col - member + lax.rem(member + step, 8))

    around = [(a, b) for a in (-1, 0, 1) for b in (-1, 0, 1) if (a, b) != (0, 0)]

    def halo_device(a, b):
        return (lax.rem(row + a + 8, 8), lax.rem(col + b + 16, 16))

    barrier = pltpu.get_barrier_semaphore()
    partners = [sibling] + [device(axis, step) for axis in "xyz" for step in (1, 2, 3)]
    partners += [group_device(step) for step in range(1, 8)]
    partners += [halo_device(a, b) for a, b in around]
    for partner in partners:
        pl.semaphore_signal(barrier, inc=1, device_id=partner, device_id_type=MESH)
    pl.semaphore_wait(barrier, len(partners))

    def remote(src, dst, send_sem, recv_sem, target):
        return pltpu.make_async_remote_copy(
            src_ref=src,
            dst_ref=dst,
            send_sem=send_sem,
            recv_sem=recv_sem,
            device_id=target,
            device_id_type=MESH,
        )

    def group_copy(step):
        other = lax.rem(member + step, 8)
        return remote(
            stage.at[other], slots.at[member], group_s.at[step - 1], group_r.at[step - 1], group_device(step)
        )

    for m in range(8):
        stage[m, 0:98, :] = shard[:, 128 * m : 128 * m + 128]
    group_copies = [group_copy(step) for step in range(1, 8)]
    for copy in group_copies:
        copy.start()

    def halo_copy(index):
        a, b = around[index]
        if b == 0:
            src, dst = feat.at[0 if a < 0 else 31], halo_row.at[0 if a > 0 else 1]
        elif a == 0:
            src, dst = edge_cols.at[0 if b < 0 else 1], halo_col.at[0 if b > 0 else 1]
        else:
            src = feat.at[0 if a < 0 else 31, pl.ds(0 if b < 0 else 16, 16)]
            dst = halo_corner.at[0 if a > 0 else 1, 0 if b > 0 else 1]
        return remote(src, dst, halo_s.at[index], halo_r.at[index], halo_device(a, b))

    halo_copies = [halo_copy(index) for index in range(8)]
    for copy in halo_copies:
        copy.start()

    def region(at, first, count):
        def one(axis):
            return slice(None) if at[axis] is None else at[axis]

        if at["x"] is None:
            low, high = slice(None), slice(None)
        else:
            low, high = lax.rem(at["x"], 2), at["x"] // 2
        return wf.at[low, one("y"), one("z"), core, high, pl.ds(first, count)]

    def held(part, phase, step):
        order = PARTS[part][3]
        at = dict(pos)
        for axis in order[:phase]:
            at[axis] = None
        at[order[phase]] = lax.rem(pos[order[phase]] + (step + 4), 4)
        return at

    def ring_copies(part, phase, half):
        first, cut, count, order = PARTS[part]
        axis = order[phase]
        copies = []
        for way, step in ((0, 1), (1, -1)):
            sem = ((part * 3 + phase) * 2 + half) * 2 + way
            if half == 0:
                ref = region(held(part, phase, 0), first, count)
            elif way == 0:
                ref = region(held(part, phase, -1), first, cut)
            else:
                ref = region(held(part, phase, 1), first + cut, count - cut)
            copies.append(remote(ref, ref, ring_s.at[sem], ring_r.at[sem], device(axis, step)))
        return copies

    def sib_copy(part, phase, step):
        first, cut, count, order = PARTS[part]
        ref = region(held(part, phase, step), first, count)
        index = part * 10 + phase * 3 + step % 4 if step else part * 10
        return remote(ref, ref, sib_s.at[index], sib_r.at[0], sibling)

    def ring_start(phase, half):
        for part in range(3):
            for copy in ring_copies(part, phase, half):
                copy.start()

    def ring_wait(phase, half):
        for part in range(3):
            for copy in ring_copies(part, phase, half):
                copy.wait_recv()

    def sib_start(phase, steps):
        for part in range(3):
            for step in steps:
                sib_copy(part, phase, step).start()

    def ring_step(index):
        phase, half = divmod(index, 2)
        ring_wait(phase, half)
        if half == 0:
            ring_start(phase, 1)
            sib_start(phase, (-1, 1))
        else:
            if phase < 2:
                ring_start(phase + 1, 0)
            sib_start(phase, (2,))

    slots[member] = stage[member]
    for copy in group_copies:
        copy.wait_recv()
    whole = jnp.concatenate([slots[m].astype(jnp.float32)[0:98] for m in range(8)], axis=0)
    wf[lax.rem(pos["x"], 2), pos["y"], pos["z"], core, pos["x"] // 2] = whole.astype(jnp.bfloat16)
    ring_start(0, 0)
    sib_start(0, (0,))

    for copy in halo_copies:
        copy.wait_recv()
    zero = jnp.float32(0)
    for a in range(2):
        inside = (row > 0) if a == 0 else (row < 7)
        ext[33 * a] = jnp.where(inside, halo_row[a].astype(jnp.float32), zero).astype(jnp.bfloat16)
        for b in range(2):
            inner = inside & ((col > 0) if b == 0 else (col < 15))
            corner = halo_corner[a, b].astype(jnp.float32)
            cell = corner[15:16] if b == 0 else corner[0:1]
            place = 7 if a == 0 else 40
            side[b, place : place + 1, :] = jnp.where(inner, cell, zero)
    for b in range(2):
        inside = (col > 0) if b == 0 else (col < 15)
        side[b, 8:40, :] = jnp.where(inside, halo_col[b].astype(jnp.float32), zero)
    ext[1:33] = feat[...]
    place = lax.broadcasted_iota(jnp.int32, (32, CH), 0)

    def tap_row(i, carry):
        centre = ext[i].astype(jnp.float32)
        left = jnp.where(place == 0, side[0, pl.ds(7 + i, 1), :], pltpu.roll(centre, 1, 0))
        right = jnp.where(place == 31, side[1, pl.ds(7 + i, 1), :], pltpu.roll(centre, 31, 0))
        taps[i, :, 0:256] = left.astype(jnp.bfloat16)
        taps[i, :, 256:512] = ext[i]
        taps[i, :, 512:768] = right.astype(jnp.bfloat16)
        return carry

    lax.fori_loop(0, 34, tap_row, 0)

    def conv_rows(i, carry):
        first = i * 8
        value = jnp.zeros((256, CH), jnp.float32)
        for a in range(3):
            value = value + dot(taps[pl.ds(first + a, 8)].reshape(256, 768), conv_w[a])
        neck[pl.ds(pl.multiple_of(i * 256, 256), 256), :] = value.astype(jnp.bfloat16)
        return carry

    lax.fori_loop(0, 4, conv_rows, 0)

    lane = lax.broadcasted_iota(jnp.int32, (ROIS, 128), 1)
    angle_hot = jnp.where(lane == meta[:, 1:2].astype(jnp.int32), 1.0, 0.0).astype(jnp.bfloat16)
    base = meta[:, 0:1]
    cell_lane = lax.broadcasted_iota(jnp.int32, (ROIS, CELLS), 1)

    def sample(k, carry):
        cells = (dot(angle_hot, table[k]) + base).astype(jnp.int32)
        for j in range(POOL):
            hot = jnp.where(cell_lane == cells[:, j : j + 1], 1.0, 0.0).astype(jnp.bfloat16)
            x[k, :, 256 * j : 256 * j + 256] = dot(hot, neck[...]).astype(jnp.bfloat16)
        for index in range(4):

            @pl.when(k == index)
            def _():
                ring_step(index)

        return carry

    lax.fori_loop(0, POOL, sample, 0)
    hot_t = jnp.where(
        lax.broadcasted_iota(jnp.int32, (128, ROIS), 0) == meta_t[1:2, :].astype(jnp.int32), 1.0, 0.0
    ).astype(jnp.bfloat16)
    cells_t[...] = (dot(table_t[...], hot_t) + meta_t[0:1, :]).astype(jnp.int32)
    ring_step(4)
    ring_step(5)
    for copy in group_copies + halo_copies:
        copy.wait_send()
    for part in range(3):
        for phase in range(3):
            for half in range(2):
                for copy in ring_copies(part, phase, half):
                    copy.wait_send()
            for step in (0, -1, 1, 2) if phase == 0 else (-1, 1, 2):
                sib_copy(part, phase, step).wait_send()
    other_core = wf.at[:, :, :, 1 - core]
    pltpu.make_async_copy(other_core, other_core, sib_r.at[0]).wait()

    flat = wf.reshape(8, GROUP * 16, 128)

    def weight(first, count, pieces=range(8)):
        return jnp.concatenate([flat[m, pl.ds(first, count), :] for m in pieces], axis=1)

    pre1[...] = jnp.zeros_like(pre1)

    def forward(k, carry):
        first = pl.multiple_of(k * SPAN, SPAN)
        for n in range(4):
            pre1[:, 256 * n : 256 * n + 256] += dot(x[k], weight(first, SPAN, (2 * n, 2 * n + 1)))
        return carry

    lax.fori_loop(0, POOL, forward, 0)

    def activate(pre, gp, hid):
        def some(i, carry):
            rows = pl.ds(pl.multiple_of(i * 32, 32), 32)
            value = pre[rows, :]
            phi = erf_parts(value)
            hid[rows, :] = (value * phi).astype(jnp.bfloat16)
            gp[rows, :] = slope(value, phi)
            return carry

        lax.fori_loop(0, ROIS // 32, some, 0)

    activate(pre1, gp1, hid1)
    for n in range(4):
        pre2[:, 256 * n : 256 * n + 256] = dot(hid1[...], w2[:, 256 * n : 256 * n + 256])
    hid2 = dpre1
    activate(pre2, gp2, hid2)
    z = dot(hid2[...], wo[...])
    label = meta[:, 2:3].astype(jnp.int32)
    live = meta[:, 3:4]
    onehot = jnp.where(lane == label, 1.0, 0.0)
    foreground = jnp.where(label < CLASSES, 1.0, 0.0)
    dlogit = 1.0 / (1.0 + jnp.exp(-(z + prior_logit))) - onehot
    dbox = jnp.clip(z - meta[...], -1.0, 1.0) * foreground
    dz = jnp.where(lane < CLASSES, dlogit, jnp.where(lane < OUTS, dbox, 0.0))
    dz = jnp.where(live > 0.5, dz, 0.0).astype(jnp.bfloat16)
    for n in range(4):
        cols = slice(256 * n, 256 * n + 256)
        dpre2[:, cols] = (dot_nt(dz, wo[cols, :]) * gp2[:, cols]).astype(jnp.bfloat16)

    mine = pl.multiple_of(core * 512, 512)
    theirs = pl.multiple_of(512 - core * 512, 512)
    for start, out in ((theirs, send0), (mine, keep)):
        hid1_half = hid1[:, pl.ds(start, 512)]
        for n in range(4):
            cols = slice(256 * n, 256 * n + 256)
            out[:, cols] = dot_tn(hid1_half, dpre2[:, cols]).astype(out.dtype)
        out[:, HID:] = dot_tn(hid2[:, pl.ds(start, 512)], dz).astype(out.dtype)
        if out is send0:
            remote(send0, recv0, red_s.at[0], red_r.at[0], sibling).start()

    for n in range(4):
        cols = slice(256 * n, 256 * n + 256)
        dpre1[:, cols] = (dot_nt(dpre2[...], w2[cols, :]) * gp1[:, cols]).astype(jnp.bfloat16)

    def order(part, level):
        return PARTS[part][3][level]

    def spot(axis, step):
        return lax.rem(pos[axis] + (step + 4), 4)

    def cols_of(part):
        return pl.ds(COLS * part, COLS)

    def scatter_copies(level, src, dst, rows, sems):
        copies = []
        for part in range(3):
            axis = order(part, level)
            for step in (1, 2, 3):
                piece = src.at[part, pl.ds(pl.multiple_of(spot(axis, step) * rows, rows), rows)]
                sem = sems + part * 3 + step - 1
                copies.append(
                    remote(piece, dst.at[part, step - 1], red_s.at[sem], red_r.at[sem], device(axis, step))
                )
        return copies

    def share_copies(sems):
        copies = []
        for part in range(3):
            axis = order(part, 2)
            for step in (1, 2, 3):
                sem = sems + part * 3 + step - 1
                spot_ref = recv3.at[part, pos[axis]]
                copies.append(remote(spot_ref, spot_ref, red_s.at[sem], red_r.at[sem], device(axis, step)))
        return copies

    def place_of(part, level):
        first = core * 512 + pos[order(part, 0)] * 128
        if level == 1:
            return pl.ds(pl.multiple_of(first + pos[order(part, 1)] * 32, 32), 32)
        return pl.ds(pl.multiple_of(first, 128), 128)

    def spread_copies(level, sems):
        copies = []
        for part in range(3):
            axis = order(part, level)
            for step in (1, 2, 3):
                sem = sems + part * 3 + step - 1
                ref = total.at[place_of(part, level), cols_of(part)]
                copies.append(remote(ref, ref, red_s.at[sem], red_r.at[sem], device(axis, step)))
        return copies

    copy0 = lambda: [remote(send0, recv0, red_s.at[0], red_r.at[0], sibling)]
    copy1 = lambda: scatter_copies(0, send1, recv1, 128, 1)
    copy2 = lambda: scatter_copies(1, send2, recv2, 32, 10)
    copy3 = lambda: share_copies(19)
    copy4 = lambda: spread_copies(1, 28)
    copy5 = lambda: spread_copies(0, 37)

    def copy6():
        ref = total.at[pl.ds(mine, 512)]
        return [remote(ref, ref, red_s.at[46], red_r.at[46], sibling)]

    def start(copies):
        for copy in copies:
            copy.start()

    def wait(copies):
        for copy in copies:
            copy.wait_recv()

    def reduce_step(index):
        if index == 0:
            wait(copy0())
            for part in range(3):
                cols = slice(COLS * part, COLS * part + COLS)

                def some(i, carry):
                    rows = pl.ds(pl.multiple_of(i * 64, 64), 64)
                    value = keep[rows, cols] + recv0[rows, cols].astype(jnp.float32)
                    keep[rows, cols] = value
                    send1[part, rows, :] = value.astype(jnp.bfloat16)
                    return carry

                lax.fori_loop(0, 8, some, 0)
            start(copy1())
        elif index == 1:
            wait(copy1())
            for part in range(3):
                cols = slice(COLS * part, COLS * part + COLS)
                own = pl.ds(pl.multiple_of(pos[order(part, 0)] * 128, 128), 128)
                value = keep[own, cols]
                for step in range(3):
                    value = value + recv1[part, step].astype(jnp.float32)
                keep1[part] = value
                send2[part] = value.astype(jnp.bfloat16)
            start(copy2())
        elif index == 2:
            wait(copy2())
            for part in range(3):
                own = pl.ds(pl.multiple_of(pos[order(part, 1)] * 32, 32), 32)
                value = keep1[part, own, :]
                for step in range(3):
                    value = value + recv2[part, step].astype(jnp.float32)
                recv3[part, pos[order(part, 2)]] = value.astype(jnp.bfloat16)
            start(copy3())
        elif index == 3:
            wait_share()
            for part in range(3):
                value = recv3[part, 0].astype(jnp.float32)
                for step in range(1, 4):
                    value = value + recv3[part, step].astype(jnp.float32)
                cols = slice(COLS * part, COLS * part + COLS)
                total[place_of(part, 1), cols] = value.astype(jnp.bfloat16)
            start(copy4())
        elif index == 4:
            wait(copy4())
            start(copy5())
        elif index == 5:
            wait(copy5())
            start(copy6())

    def wait_share():
        wait(copy3())

    feat_grad[...] = jnp.zeros_like(feat_grad)
    cell_row = lax.broadcasted_iota(jnp.int32, (256, ROIS), 0)

    def backward(k, carry):
        for j in range(POOL):
            first = pl.multiple_of(k * SPAN + 256 * j, 256)
            dxs[256 * j : 256 * j + 256, :] = dot_nt(dpre1[...], weight(first, 256)).astype(jnp.bfloat16)
        for q in range(4):
            for j in range(POOL):
                cells = cells_t[pl.ds(k * POOL + j, 1), :] - 256 * q
                x[q, :, 256 * j : 256 * j + 256] = jnp.where(cell_row == cells, 1.0, 0.0).astype(jnp.bfloat16)
            feat_grad[256 * q : 256 * q + 256, :] += dot(x[q], dxs[...])
        for index in range(6):

            @pl.when(k == index)
            def _():
                reduce_step(index)

        return carry

    lax.fori_loop(0, POOL, backward, 0)
    wait(copy6())
    for make in (copy0, copy1, copy2, copy3, copy4, copy5, copy6):
        for copy in make():
            copy.wait_send()


def on_device(
    features,
    conv_weight,
    first_weight,
    second_weight,
    out_weight,
    roi_count,
    roi_row,
    roi_col,
    roi_angle,
    roi_label,
    roi_target,
):
    f32, bf16 = jnp.float32, jnp.bfloat16
    shift_rows, shift_cols = offset_tables(POOL, ANGLES)
    shift = (shift_rows * 32 + shift_cols).astype(np.float32)
    table = np.zeros((POOL, 128, 128), np.float32)
    table[:, :ANGLES, :POOL] = shift.reshape(ANGLES, POOL, POOL).transpose(1, 0, 2)
    table_t = np.zeros((64, 128), np.float32)
    table_t[:SAMPLES, :ANGLES] = shift.T
    live = jnp.arange(ROIS, dtype=jnp.int32) < roi_count[0]
    facts = [(roi_row * 32 + roi_col), roi_angle, roi_label, live]
    facts = [fact.astype(f32) for fact in facts]
    meta = jnp.concatenate(
        [
            jnp.stack(facts, axis=1),
            jnp.zeros((ROIS, CLASSES - 4), f32),
            roi_target.astype(f32),
            jnp.zeros((ROIS, 128 - OUTS), f32),
        ],
        axis=1,
    )
    meta_t = jnp.stack(facts[:2] + [jnp.zeros((ROIS,), f32)] * 6, axis=0)
    edge_cols = jnp.stack([features[:, 0], features[:, 31]])
    out_wide = jnp.pad(out_weight, ((0, 0), (0, 128 - OUTS)))

    vmem = pl.BlockSpec(memory_space=pltpu.VMEM)
    dma = pltpu.SemaphoreType.DMA
    neck, feat_grad, total = pl.pallas_call(
        kernel,
        out_shape=(
            jax.ShapeDtypeStruct((CELLS, CH), bf16),
            jax.ShapeDtypeStruct((CELLS, CH), f32),
            jax.ShapeDtypeStruct((HID, WIDE), bf16),
        ),
        in_specs=[vmem] * 10,
        out_specs=(vmem, vmem, vmem),
        scratch_shapes=[
            pltpu.VMEM((2, 4, 4, 2, 2, GROUP, 128), bf16),
            pltpu.VMEM((8, 112, 128), bf16),
            pltpu.VMEM((8, 112, 128), bf16),
            pltpu.VMEM((2, 32, CH), bf16),
            pltpu.VMEM((2, 32, CH), bf16),
            pltpu.VMEM((2, 2, 16, CH), bf16),
            pltpu.VMEM((2, 48, CH), f32),
            pltpu.VMEM((34, 32, CH), bf16),
            pltpu.VMEM((34, 32, 3 * CH), bf16),
            pltpu.VMEM((POOL, ROIS, SPAN), bf16),
            pltpu.VMEM((64, ROIS), jnp.int32),
            pltpu.VMEM((ROIS, HID), f32),
            pltpu.VMEM((ROIS, HID), f32),
            pltpu.VMEM((ROIS, HID), f32),
            pltpu.VMEM((ROIS, HID), f32),
            pltpu.VMEM((ROIS, HID), bf16),
            pltpu.VMEM((ROIS, HID), bf16),
            pltpu.VMEM((ROIS, HID), bf16),
            pltpu.VMEM((SPAN, CH), bf16),
            pltpu.VMEM((512, WIDE), f32),
            pltpu.VMEM((512, WIDE), bf16),
            pltpu.VMEM((512, WIDE), bf16),
            pltpu.VMEM((3, 512, COLS), bf16),
            pltpu.VMEM((3, 3, 128, COLS), bf16),
            pltpu.VMEM((3, 128, COLS), f32),
            pltpu.VMEM((3, 128, COLS), bf16),
            pltpu.VMEM((3, 3, 32, COLS), bf16),
            pltpu.VMEM((3, 32, COLS), f32),
            pltpu.VMEM((3, 4, 32, COLS), bf16),
            dma((8,)),
            dma((8,)),
            dma((7,)),
            dma((7,)),
            dma((36,)),
            dma((36,)),
            dma((30,)),
            dma((1,)),
            dma((47,)),
            dma((47,)),
        ],
        compiler_params=pltpu.CompilerParams(
            collective_id=0, has_side_effects=True, vmem_limit_bytes=60 * 2**20
        ),
    )(
        features,
        edge_cols,
        conv_weight.reshape(3, 3 * CH, CH),
        first_weight,
        second_weight,
        out_wide,
        meta,
        meta_t,
        jnp.asarray(table, bf16),
        jnp.asarray(table_t, bf16),
    )
    return (
        neck.reshape(32, 32, CH),
        feat_grad.reshape(32, 32, CH),
        total[:, :HID].astype(f32),
        total[:, HID : HID + OUTS].astype(f32),
    )


def solution(mesh):
    in_specs = (
        P("row", "col", None),
        P(),
        P(("row", "col"), None),
        P(),
        P(),
        P(("row", "col")),
        P(("row", "col")),
        P(("row", "col")),
        P(("row", "col")),
        P(("row", "col")),
        P(("row", "col"), None),
    )
    out_specs = (P("row", "col", None), P("row", "col", None), P(), P())
    return jax.shard_map(
        on_device, mesh=mesh, in_specs=in_specs, out_specs=out_specs, check_vma=False
    )
```

time: 393 us -> 144 us (0.37)
  waiting for transfers between devices: 213 us -> 0 us
  Pallas kernels: 0 us -> 127 us
  matrix products: 72 us -> 0 us
  local copies, waits for them, and re-layouts: 74.5 us -> 6.95 us
  between operations: 15 us -> 1.41 us
  starting transfers between devices: 11.4 us -> 0 us
  other arithmetic: 4.36 us -> 8.54 us
    psum x1 -> x0, waiting for transfers between devices: 157 us -> none  [on_device(): second_grad, out_grad = lax.psum((second_sum, out_sum), ('row', 'col'))]
    pallas_call x0 -> x1, Pallas kernels: none -> 127 us  [on_device(): pl.pallas_call(kernel, out_shape=(jax.ShapeDtypeStruct((CELLS, CH), bf16)...]
    dot_general x20 -> x0, matrix products: 72 us -> none  [the longest x2 20.1 us: add_group(): lax.dot_general(onehot, rows, (((0,), (0,)), ((), ())), preferred_element...]
    all_gather x1 -> x0, waiting for transfers between devices: 53.3 us -> none  [on_device(): lax.all_gather(first_weight, ('row', 'col'), axis=0, tiled=True)]
    unnamed x28 -> x10, local copies, waits for them, and re-layouts: 38.8 us -> 2.83 us
    reshape x2 -> x0, local copies, waits for them, and re-layouts: 26.2 us -> none  [the longest x1 13.8 us: spread_grads(): dblocks.reshape(slots // step_rows, step_rows * POOL * POOL, channels)]
    ppermute x4 -> x0, starting transfers between devices: 11.3 us -> none  [the longest x2 6.73 us: extended(): before = lax.ppermute(last, axis, up)]
    convert_element_type x2 -> x6, other arithmetic: 0.76 us -> 7.25 us  [the longest x1 4.19 us: on_device(): total[:, :HID].astype(f32)]
  transfers between devices with their start and end apart: 6 -> 0, of which waited for: 3 -> 0; matrix products, arithmetic and copies ran while one was open for 18% -> 0% of each run, Pallas kernels for 0% -> 0%
where the time goes in v1:
time: 144 us
  Pallas kernels  127 us (88%)
  other arithmetic  8.54 us (6%)
  local copies, waits for them, and re-layouts  6.95 us (5%)
    pallas_call x1, Pallas kernels, on_device(): pl.pallas_call(kernel, out_shape=(jax.ShapeDtypeStruct((CELLS, CH), bf16)...  127 us
    convert_element_type x1, other arithmetic, on_device(): total[:, :HID].astype(f32)  4.19 us

profile of v1, /device:TPU:1, one launch (start us, length us, event | category | flops | bytes accessed | tf_op | source)
XLA Modules:
  0.0 143.5 jit_solution(18441589338502710817)
XLA Ops:
  0.6 0.0 copy-start.2
  1.3 0.1 pad.8.clone
  1.4 0.1 pad.7.clone
  1.5 0.7 add_convert_fusion
  2.2 0.7 convert_element_type.31
  2.9 0.7 convert_element_type.32
  3.5 0.7 maximum_maximum_fusion.meta_t
  4.2 1.0 fusion.1
  5.3 0.6 pad_maximum_fusion.edge_cols
  5.9 0.1 copy.27
  6.0 0.1 copy.26
  6.2 0.1 copy.25
  6.3 0.8 copy.28
  7.2 0.9 concatenate.3.meta
  8.1 0.0 copy-done.2
  8.1 0.2 copy.24
  8.3 0.8 pad.4.wo
  9.1 126.6 %shard_map.156 = (bf16[1024,256]{1,0:T(8,128)(2,1)}, f32[1024,256]{1,0:T(8,128)}, bf16[1024,1152]{1,0:T(8,128)(2,1)}) custom-call(bf16[32,32,256]{2,1,0:T(8,128)(2,1)} %feat.1, bf16[2,32,256]{2,1,0:T(8,128)(2,1)} %pad_maximum_fusion.edge_cols, bf16[3,768,256]{2,1,0:T(8,128)(2,1)} %bitcast.14, bf16[98,1024]{1,0:T(8,128)(2,1)} %shard.1, ...), custom_call_target="tpu_custom_call" | custom-call | tf_op jit(solution)/shard_map/pallas_call | solution.py:581
  135.7 1.0 slice_convert_fusion.1
  136.7 0.9 copy.29
  137.6 0.0 copy-start.1
  137.6 0.0 copy-start
  137.6 4.2 %slice_convert_fusion = f32[1024,1024]{1,0:T(8,128)} fusion(bf16[1024,1152]{1,0:T(8,128)(2,1)} %get-tuple-element.9), kind=kLoop, calls=%fused_computation | loop fusion | flops 1048576 | bytes 6291456 | tf_op jit(solution)/shard_map/convert_element_type | solution.py:649
  141.8 0.0 copy-done.1
  141.8 0.8 copy.37
  142.5 0.0 copy-done
  142.5 1.0 copy.38
  (6 shorter events, 0.1 us)
Async XLA Ops:
  0.6 7.5 %copy-start.2 = (bf16[1024,42]{0,1:T(8,128)(2,1)S(1)}, bf16[1024,42]{0,1:T(8,128)(2,1)}, u32[]{:S(2)}) copy-start(bf16[1024,42]{0,1:T(8,128)(2,1)} %param.17) | copy-start | bytes 258052
  137.6 4.2 %copy-start.1 = (bf16[1024,256]{1,0:T(8,128)(2,1)S(1)}, bf16[1024,256]{1,0:T(8,128)(2,1)}, u32[]{:S(2)}) copy-start(bf16[1024,256]{1,0:T(8,128)(2,1)} %get-tuple-element.7) | copy-start | bytes 1572868
  137.6 5.0 %copy-start = (f32[1024,256]{1,0:T(8,128)S(1)}, f32[1024,256]{1,0:T(8,128)}, u32[]{:S(2)}) copy-start(f32[1024,256]{1,0:T(8,128)} %get-tuple-element.8) | copy-start | bytes 3145732

commit v2 on v1

v2 whole, which is shorter than its diff:
```python
import heapq
import math

import jax
import jax.numpy as jnp
import numpy as np
from jax import lax
from jax.experimental import pallas as pl
from jax.experimental.pallas import tpu as pltpu
from jax.sharding import PartitionSpec as P

POOL = 7
ANGLES = 8
CLASSES = 37
OUTS = 42
HID = 1024
CH = 256
CELLS = 1024
ROIS = 256
SAMPLES = POOL * POOL
GROUP = 784
SPAN = POOL * CH
WIDE = HID + 128
COLS = WIDE // 3
MESH = pl.DeviceIdType.MESH
SLOTS = (0, 5, 7, 9, 11)

prior_logit = -4.59512

PARTS = (
    (0, 128, 256, "xyz"),
    (256, 128, 256, "yzx"),
    (512, 144, 272, "zxy"),
)


LINK = 46.5e3
DELAY = 2.2


def arrivals():
    free, events, got, order, count = {}, [], set(), [], 0
    waiting = {axis: [] for axis in "xyz"}
    opened = set()

    def push(now, axis, way, size, item):
        nonlocal count
        end = max(now, free.get((axis, way), 0.0)) + size / LINK
        free[(axis, way)] = end
        count += 1
        heapq.heappush(events, (end + DELAY, count, item))

    def send(now, item):
        part, phase, key, half, way = item
        first, cut, rows, axes = PARTS[part]
        part_rows = rows if half == 0 else cut if way == 0 else rows - cut
        push(now, axes[phase], way, part_rows * 256 * (4 if phase == 2 else 1), item)

    for item in first_sends():
        send(0.0, item)
    while events:
        now, _, item = heapq.heappop(events)
        got.add(item)
        order.append((now, item))
        for after in follow(item, got, waiting, opened):
            send(now, after)
    return order


def both(part, phase, key):
    return [(part, phase, key, 0, 0), (part, phase, key, 0, 1)]


def first_sends():
    return [item for phase in (0, 1) for part in range(3) for item in both(part, phase, 0)]


def follow(item, got, waiting, opened):
    part, phase, key, half, way = item
    sends = [(part, phase, key, 1, way)] if half == 0 else []
    lines = []
    if phase == 0:
        if half == 0:
            sends += both(part, 1, -1 if way == 0 else 1)
        elif (part, 0, 0, 1, 1 - way) in got:
            sends += both(part, 1, 2)
            lines.append(0)
    elif phase == 1:
        offsets = (0, -1, 1, 2)
        if half == 0 and all((part, 1, k, 0, way) in got for k in offsets):
            lines.append(-1 if way == 0 else 1)
        if half == 1 and all((part, 1, k, 1, w) in got for k in offsets for w in (0, 1)):
            lines.append(2)
    for line in lines:
        axis = PARTS[part][3][2]
        if axis in opened:
            sends += both(part, 2, line)
        else:
            waiting[axis].append((part, line))
    if phase == 1:
        axis = PARTS[part][3][1]
        if axis not in opened and all((part, 1, k, 0, w) in got for k in (0, -1, 1, 2) for w in (0, 1)):
            opened.add(axis)
            for other, line in waiting[axis]:
                sends += both(other, 2, line)
    return sends


def offset_tables(pool, angles):
    turn = np.arange(angles) * math.pi / angles
    along = np.arange(pool) - pool // 2
    down = (along[:, None] * np.ones((1, pool))).reshape(1, -1)
    across = (np.ones((pool, 1)) * along[None, :]).reshape(1, -1)
    cosine = np.cos(turn)[:, None]
    sine = np.sin(turn)[:, None]
    shift_rows = np.floor(down * cosine - across * sine + 0.5).astype(np.int32)
    shift_cols = np.floor(down * sine + across * cosine + 0.5).astype(np.int32)
    return (shift_rows, shift_cols)


def erf_parts(value):
    return 0.5 * (1.0 + lax.erf(value * math.sqrt(0.5)))


def slope(value, phi):
    return phi + value * jnp.exp(-0.5 * value * value) * (1.0 / math.sqrt(2.0 * math.pi))


def dot(a, b):
    return jnp.dot(a, b, preferred_element_type=jnp.float32)


def dot_nt(a, b):
    return lax.dot_general(a, b, (((1,), (1,)), ((), ())), preferred_element_type=jnp.float32)


def dot_tn(a, b):
    return lax.dot_general(a, b, (((0,), (0,)), ((), ())), preferred_element_type=jnp.float32)


def kernel(
    feat,
    conv_hbm,
    shard,
    w2_hbm,
    out_w,
    count,
    roi_row,
    roi_col,
    roi_angle,
    roi_label,
    roi_target,
    table,
    table_t,
    neck_hbm,
    grad_hbm,
    total_hbm,
    neck,
    feat_grad,
    total,
    wf,
    conv_w,
    w2,
    wo,
    facts,
    meta,
    edges,
    edge_cols,
    stage,
    slots,
    halo_row,
    halo_col,
    halo_corner,
    side,
    ext,
    taps,
    xg,
    xt,
    window,
    cells_all,
    cells_t,
    pre1,
    gp1,
    gp2,
    hid1,
    dpre2,
    dpre1,
    dxs,
    keep,
    send0,
    recv0,
    send1,
    recv1,
    keep1,
    send2,
    recv2,
    recv3,
    halo_s,
    halo_r,
    group_s,
    group_r,
    ring_s,
    ring_r,
    sib_s,
    sib_r,
    red_s,
    red_r,
    in_s,
    out_s,
):
    row = lax.axis_index("row")
    col = lax.axis_index("col")
    pos = {"x": col // 4, "y": lax.rem(col, 4), "z": row // 2}
    core = lax.rem(row, 2)

    def device(axis, step):
        at = dict(pos)
        at[axis] = lax.rem(pos[axis] + (step + 4), 4)
        return (at["z"] * 2 + core, at["x"] * 4 + at["y"])

    sibling = (row + 1 - 2 * core, col)
    member = lax.rem(col, 8)

    def group_device(step):
        return (row, col - member + lax.rem(member + step, 8))

    around = [(a, b) for a in (-1, 0, 1) for b in (-1, 0, 1) if (a, b) != (0, 0)]

    def halo_device(a, b):
        return (lax.rem(row + a + 8, 8), lax.rem(col + b + 16, 16))

    barrier = pltpu.get_barrier_semaphore()
    partners = [sibling] + [device(axis, step) for axis in "xz" for step in (1, 3)]
    partners += [group_device(step) for step in range(1, 8)]
    partners += [halo_device(a, b) for a, b in around]
    for partner in partners:
        pl.semaphore_signal(barrier, inc=1, device_id=partner, device_id_type=MESH)
    pl.semaphore_wait(barrier, len(partners))

    def remote(src, dst, send_sem, recv_sem, target):
        return pltpu.make_async_remote_copy(
            src_ref=src,
            dst_ref=dst,
            send_sem=send_sem,
            recv_sem=recv_sem,
            device_id=target,
            device_id_type=MESH,
        )

    loads = [
        pltpu.make_async_copy(conv_hbm, conv_w, in_s.at[0]),
        pltpu.make_async_copy(w2_hbm, w2, in_s.at[1]),
    ]
    stores = [
        pltpu.make_async_copy(neck, neck_hbm, out_s.at[0]),
        pltpu.make_async_copy(feat_grad, grad_hbm, out_s.at[1]),
        pltpu.make_async_copy(total, total_hbm, out_s.at[2]),
    ]
    for load in loads:
        load.start()

    def group_copy(step):
        other = lax.rem(member + step, 8)
        return remote(
            stage.at[other], slots.at[member], group_s.at[step - 1], group_r.at[step - 1], group_device(step)
        )

    for m in range(8):
        stage[m, 0:98, :] = shard[:, 128 * m : 128 * m + 128]
    group_copies = [group_copy(step) for step in range(1, 8)]
    for copy in group_copies:
        copy.start()

    for i in range(32):
        cells_in_row = feat[i].astype(jnp.float32)
        edges[0, i : i + 1, :] = cells_in_row[0:1]
        edges[1, i : i + 1, :] = cells_in_row[31:32]
    edge_cols[...] = edges[...].astype(jnp.bfloat16)

    def halo_copy(index):
        a, b = around[index]
        if b == 0:
            src, dst = feat.at[0 if a < 0 else 31], halo_row.at[0 if a > 0 else 1]
        elif a == 0:
            src, dst = edge_cols.at[0 if b < 0 else 1], halo_col.at[0 if b > 0 else 1]
        else:
            src = feat.at[0 if a < 0 else 31, pl.ds(0 if b < 0 else 16, 16)]
            dst = halo_corner.at[0 if a > 0 else 1, 0 if b > 0 else 1]
        return remote(src, dst, halo_s.at[index], halo_r.at[index], halo_device(a, b))

    halo_copies = [halo_copy(index) for index in range(8)]
    for copy in halo_copies:
        copy.start()

    def region(at, first, count):
        def one(axis):
            return slice(None) if at[axis] is None else at[axis]

        if at["x"] is None:
            low, high = slice(None), slice(None)
        else:
            low, high = lax.rem(at["x"], 2), at["x"] // 2
        return wf.at[low, one("y"), one("z"), core, high, pl.ds(first, count)]

    def spot(axis, step):
        return lax.rem(pos[axis] + (step + 4), 4)

    def item_copy(item):
        part, phase, key, half, way = item
        first, cut, rows, axes = PARTS[part]
        at = dict(pos)
        if phase == 1:
            at[axes[0]] = spot(axes[0], key)
        if phase == 2:
            at[axes[0]] = None
            at[axes[1]] = spot(axes[1], key)
        axis = axes[phase]
        if half == 1:
            at[axis] = spot(axis, -1 if way == 0 else 1)
            first, rows = (first, cut) if way == 0 else (first + cut, rows - cut)
        ref = region(at, first, rows)
        sem = part * 36 + (phase * 16 - 12 if phase else 0) + (key % 4) * 4 + half * 2 + way
        return remote(ref, ref, ring_s.at[sem], ring_r.at[sem], device(axis, 1 if way == 0 else -1))

    def line_copy(part, near, far):
        first, cut, rows, axes = PARTS[part]
        at = {axes[0]: None, axes[1]: spot(axes[1], near), axes[2]: spot(axes[2], far)}
        ref = region(at, first, rows)
        index = part * 4 + far % 4
        return remote(ref, ref, sib_s.at[index * 4 + near % 4], sib_r.at[index], sibling)

    def line_wait(part, far):
        first, cut, rows, axes = PARTS[part]
        at = {axes[0]: None, axes[1]: None, axes[2]: spot(axes[2], far)}
        ref = region(at, first, rows)
        pltpu.make_async_copy(ref, ref, sib_r.at[part * 4 + far % 4]).wait()

    got, waiting, opened = set(), {axis: [] for axis in "xyz"}, set()

    def arrive(item):
        item_copy(item).wait_recv()
        got.add(item)
        for after in follow(item, got, waiting, opened):
            item_copy(after).start()
        part, phase, key, half, way = item
        offsets = (0, -1, 1, 2)
        if phase == 0 and half == 1 and (part, 0, 0, 1, 1 - way) in got:
            line_copy(part, 0, 0).start()
        if phase == 1 and half == 0 and all((part, 1, k, 0, way) in got for k in offsets):
            line_copy(part, -1 if way == 0 else 1, 0).start()
        if phase == 1 and half == 1 and all((part, 1, k, 1, w) in got for k in offsets for w in (0, 1)):
            line_copy(part, 2, 0).start()
        if phase == 2 and half == 0:
            line_copy(part, key, -1 if way == 0 else 1).start()
        if phase == 2 and half == 1 and (part, 2, key, 1, 1 - way) in got:
            line_copy(part, key, 2).start()

    facts[...] = jnp.zeros_like(facts)
    position = lax.broadcasted_iota(jnp.int32, (1, ROIS), 1)
    angle_row = roi_angle[...].reshape(1, ROIS)
    base_row = roi_row[...].reshape(1, ROIS) * 32 + roi_col[...].reshape(1, ROIS)
    facts[0:1, :] = base_row.astype(jnp.float32)
    facts[1:2, :] = angle_row.astype(jnp.float32)
    facts[2:3, :] = roi_label[...].reshape(1, ROIS).astype(jnp.float32)
    facts[3:4, :] = jnp.where(position < count[0], 1.0, 0.0)
    facts[CLASSES:OUTS, :] = roi_target[...].astype(jnp.float32)
    meta[...] = facts[...].T
    wo[...] = jnp.zeros_like(wo)
    wo[0:OUTS, :] = out_w[...]
    lane = lax.broadcasted_iota(jnp.int32, (ROIS, 128), 1)
    angle_hot = jnp.where(lane == meta[:, 1:2].astype(jnp.int32), 1.0, 0.0).astype(jnp.bfloat16)
    cells_all[...] = dot(angle_hot, table[...]) + meta[:, 0:1]
    hot_t = jnp.where(lax.broadcasted_iota(jnp.int32, (128, ROIS), 0) == angle_row, 1.0, 0.0)
    cells_t[...] = dot(table_t[...], hot_t.astype(jnp.bfloat16)).astype(jnp.int32) + base_row

    slots[member] = stage[member]
    for copy in group_copies:
        copy.wait_recv()
    whole = jnp.concatenate([slots[m].astype(jnp.float32)[0:98] for m in range(8)], axis=0)
    wf[lax.rem(pos["x"], 2), pos["y"], pos["z"], core, pos["x"] // 2] = whole.astype(jnp.bfloat16)
    for item in first_sends():
        item_copy(item).start()

    loads[0].wait()
    for copy in halo_copies:
        copy.wait_recv()
    zero = jnp.float32(0)
    for a in range(2):
        inside = (row > 0) if a == 0 else (row < 7)
        ext[33 * a] = jnp.where(inside, halo_row[a].astype(jnp.float32), zero).astype(jnp.bfloat16)
        for b in range(2):
            inner = inside & ((col > 0) if b == 0 else (col < 15))
            corner = halo_corner[a, b].astype(jnp.float32)
            cell = corner[15:16] if b == 0 else corner[0:1]
            place = 7 if a == 0 else 40
            side[b, place : place + 1, :] = jnp.where(inner, cell, zero)
    for b in range(2):
        inside = (col > 0) if b == 0 else (col < 15)
        side[b, 8:40, :] = jnp.where(inside, halo_col[b].astype(jnp.float32), zero)
    ext[1:33] = feat[...]
    place = lax.broadcasted_iota(jnp.int32, (32, CH), 0)

    def tap_row(i, carry):
        centre = ext[i].astype(jnp.float32)
        left = jnp.where(place == 0, side[0, pl.ds(7 + i, 1), :], pltpu.roll(centre, 1, 0))
        right = jnp.where(place == 31, side[1, pl.ds(7 + i, 1), :], pltpu.roll(centre, 31, 0))
        taps[i, :, 0:256] = left.astype(jnp.bfloat16)
        taps[i, :, 256:512] = ext[i]
        taps[i, :, 512:768] = right.astype(jnp.bfloat16)
        return carry

    lax.fori_loop(0, 34, tap_row, 0)

    def conv_rows(i, carry):
        first = i * 8
        value = jnp.zeros((256, CH), jnp.float32)
        for a in range(3):
            value = value + dot(taps[pl.ds(first + a, 8)].reshape(256, 768), conv_w[a])
        neck[pl.ds(pl.multiple_of(i * 256, 256), 256), :] = value.astype(jnp.bfloat16)
        return carry

    lax.fori_loop(0, 4, conv_rows, 0)
    stores[0].start()

    cell_lane = lax.broadcasted_iota(jnp.int32, (ROIS, CELLS), 1)

    def picked(cells, j):
        hot = jnp.where(cell_lane == cells[:, j : j + 1].astype(jnp.int32), 1.0, 0.0).astype(jnp.bfloat16)
        return dot(hot, neck[...])

    window[:, 0:256] = picked(cells_all[...], 0)
    xt[...] = jnp.zeros_like(xt)
    group_lane = lax.broadcasted_iota(jnp.int32, (ROIS, CH), 1) // 16

    def sample(g):
        cells = pltpu.roll(cells_all[...], 127 - 3 * g, 1)
        for j in range(3):
            window[:, 256 + 256 * j : 512 + 256 * j] = picked(cells, j)
        last = window[:, 768:1024]
        xt[...] = jnp.where(group_lane == g, last.astype(jnp.bfloat16), xt[...])
        far = g // 8
        shift = 16 * lax.rem(g, 8)
        back = lax.rem(128 - shift, 128)
        for i in range(6):
            low = pltpu.roll(window[:, pl.ds(pl.multiple_of(128 * (far + i), 128), 128)], back, 1)
            high = pltpu.roll(window[:, pl.ds(pl.multiple_of(128 * (far + i + 1), 128), 128)], back, 1)
            place = pl.ds(pl.multiple_of(768 * lax.rem(g, 2) + 128 * i, 128), 128)
            xg[g // 2, :, place] = jnp.where(lane < 128 - shift, low, high).astype(jnp.bfloat16)
        window[:, 0:256] = last

    def entries(z, c, high, first):
        return xg[z * 2 + c, :, pl.ds(pl.multiple_of(768 * high + first, 256), 256)]

    def product(part, far):
        axis = PARTS[part][3][2]
        here = spot(axis, far)
        line_wait(part, far)
        if axis == "z":
            pairs = [(c, high) for c in range(2) for high in range(2)]
            left = jnp.concatenate([entries(here, c, high, 0) for c, high in pairs], axis=1)
            for n in range(4):
                low, y = n // 2, 2 * (n % 2)
                halves = [
                    jnp.concatenate([wf[low, y + i, here, c, high, 0:256, :] for c, high in pairs], axis=0)
                    for i in range(2)
                ]
                pre1[:, 256 * n : 256 * n + 256] += dot(left, jnp.concatenate(halves, axis=1))
        elif axis == "x":
            low, high = lax.rem(here, 2), here // 2
            for z in range(0, 4, 2):
                pairs = [(z + i, c) for i in range(2) for c in range(2)]
                left = jnp.concatenate([entries(a, c, high, 256) for a, c in pairs], axis=1)
                for n in range(2):
                    halves = [
                        jnp.concatenate([wf[low, 2 * n + i, a, c, high, 256:512, :] for a, c in pairs], axis=0)
                        for i in range(2)
                    ]
                    cols = pl.ds(pl.multiple_of(512 * low + 256 * n, 256), 256)
                    pre1[:, cols] += dot(left, jnp.concatenate(halves, axis=1))
        else:

            def some(z, carry):
                pairs = [(c, high) for c in range(2) for high in range(2)]
                left = jnp.concatenate([entries(z, c, high, 512) for c, high in pairs], axis=1)
                halves = [
                    jnp.concatenate([wf[low, here, z, c, high, 512:768, :] for c, high in pairs], axis=0)
                    for low in range(2)
                ]
                add(dot(left, jnp.concatenate(halves, axis=1)))
                return carry

            def add(value):
                for low in range(2):
                    cols = pl.ds(pl.multiple_of(512 * low + 128 * here, 128), 128)
                    pre1[:, cols] += value[:, 128 * low : 128 * low + 128]

            lax.fori_loop(0, 4, some, 0)
            groups = [(z, c, high) for z in range(4) for c in range(2) for high in range(2)]
            halves = [
                jnp.concatenate([wf[low, here, z, c, high, 768:784, :] for z, c, high in groups], axis=0)
                for low in range(2)
            ]
            add(dot(xt[...], jnp.concatenate(halves, axis=1)))

    events = arrivals()
    now = 3.0
    batches = []
    for g in range(16):
        batches.append([])
        while events and events[0][0] <= now + 0.5:
            time, item = events.pop(0)
            now = max(now + 0.05, time)
            batches[-1].append(item)
        now += 1.1
    pre1[...] = jnp.zeros_like(pre1)

    def sample_step(g, carry):
        for index, batch in enumerate(batches):
            if batch:

                @pl.when(g == index)
                def _(batch=batch):
                    for item in batch:
                        arrive(item)

        sample(g)
        return carry

    lax.fori_loop(0, 16, sample_step, 0)
    due = {}
    for time, item in arrivals():
        part, phase, key, half, way = item
        far = 0 if phase < 2 else 2 if half else -1 if way == 0 else 1
        due[(part, far)] = max(due.get((part, far), 0.0), time + 3.0)
    todo = sorted((time, key) for key, time in due.items())
    while todo or events:
        if events and (events[0][0] <= now + 0.3 or not todo):
            time, item = events.pop(0)
            now = max(now + 0.05, time)
            arrive(item)
        elif todo and (todo[0][0] <= now or not events):
            product(*todo.pop(0)[1])
            now += 0.7
        else:
            now = min(events[0][0], todo[0][0])
    for copy in group_copies + halo_copies:
        copy.wait_send()
    for part in range(3):
        for phase in range(3):
            for key in (0, -1, 1, 2) if phase else (0,):
                for half in range(2):
                    for way in range(2):
                        item_copy((part, phase, key, half, way)).wait_send()
        for near in (0, -1, 1, 2):
            for far in (0, -1, 1, 2):
                line_copy(part, near, far).wait_send()
    loads[1].wait()

    flat = wf.reshape(8, GROUP * 16, 128)

    def weight(first, count):
        return jnp.concatenate([flat[m, pl.ds(first, count), :] for m in range(8)], axis=1)

    def activate(pre, hid, gp):
        def some(i, carry):
            rows = pl.ds(pl.multiple_of(i * 32, 32), 32)
            value = pre[rows, :]
            phi = erf_parts(value)
            if hid is not None:
                hid[rows, :] = (value * phi).astype(jnp.bfloat16)
            if gp is not None:
                gp[rows, :] = slope(value, phi)
            return carry

        lax.fori_loop(0, ROIS // 32, some, 0)

    activate(pre1, hid1, None)
    pre2 = window
    for n in range(4):
        pre2[:, 256 * n : 256 * n + 256] = dot(hid1[...], w2[:, 256 * n : 256 * n + 256])
    hid2 = dpre1
    activate(pre2, hid2, gp2)
    z = dot_nt(hid2[...], wo[...])
    label = meta[:, 2:3].astype(jnp.int32)
    live = meta[:, 3:4]
    onehot = jnp.where(lane == label, 1.0, 0.0)
    foreground = jnp.where(label < CLASSES, 1.0, 0.0)
    dlogit = 1.0 / (1.0 + jnp.exp(-(z + prior_logit))) - onehot
    dbox = jnp.clip(z - meta[...], -1.0, 1.0) * foreground
    dz = jnp.where(lane < CLASSES, dlogit, jnp.where(lane < OUTS, dbox, 0.0))
    dz = jnp.where(live > 0.5, dz, 0.0).astype(jnp.bfloat16)
    for n in range(4):
        cols = slice(256 * n, 256 * n + 256)
        dpre2[:, cols] = (dot(dz, wo[:, cols]) * gp2[:, cols]).astype(jnp.bfloat16)

    mine = pl.multiple_of(core * 512, 512)
    theirs = pl.multiple_of(512 - core * 512, 512)

    def half_grad(start, cols):
        if cols.stop <= HID:
            return dot_tn(hid1[:, pl.ds(start, 512)], dpre2[:, cols])
        return jnp.concatenate(
            [
                dot_tn(hid1[:, pl.ds(start, 512)], dpre2[:, cols.start : HID]),
                dot_tn(hid2[:, pl.ds(start, 512)], dz),
            ],
            axis=1,
        )

    def copy0(part):
        return [remote(send0.at[part], recv0.at[part], red_s.at[part], red_r.at[part], sibling)]

    for part in range(3):
        send0[part] = half_grad(theirs, slice(COLS * part, COLS * part + COLS)).astype(jnp.bfloat16)
        copy0(part)[0].start()
    for part in range(3):
        keep[part] = half_grad(mine, slice(COLS * part, COLS * part + COLS))
    activate(pre1, None, gp1)

    for n in range(4):
        cols = slice(256 * n, 256 * n + 256)
        dpre1[:, cols] = (dot_nt(dpre2[...], w2[cols, :]) * gp1[:, cols]).astype(jnp.bfloat16)

    def order(part, level):
        return PARTS[part][3][level]

    def cols_of(part):
        return pl.ds(COLS * part, COLS)

    def scatter_copies(part, level, src, dst, rows, sems):
        copies = []
        axis = order(part, level)
        for step in (1, 3, 2):
            piece = src.at[part, pl.ds(pl.multiple_of(spot(axis, step) * rows, rows), rows)]
            sem = sems + part * 3 + step - 1
            copies.append(remote(piece, dst.at[part, step - 1], red_s.at[sem], red_r.at[sem], device(axis, step)))
        return copies

    def copy1(part):
        return scatter_copies(part, 0, send1, recv1, 128, 3)

    def copy2(part):
        return scatter_copies(part, 1, send2, recv2, 32, 12)

    def copy3(part):
        copies = []
        axis = order(part, 2)
        for step in (1, 3, 2):
            sem = 21 + part * 3 + step - 1
            ref = recv3.at[part, pos[axis]]
            copies.append(remote(ref, ref, red_s.at[sem], red_r.at[sem], device(axis, step)))
        return copies

    def rows_at(part, step):
        return pl.ds(pl.multiple_of(core * 512 + spot(order(part, 0), step) * 128, 128), 128)

    def rows_own(part):
        first = core * 512 + pos[order(part, 0)] * 128 + pos[order(part, 1)] * 32
        return pl.ds(pl.multiple_of(first, 32), 32)

    def spread_copies(part, level, rows, sems):
        copies = []
        axis = order(part, level)
        for step in (1, 3, 2):
            sem = sems + part * 3 + step - 1
            ref = total.at[rows, cols_of(part)]
            copies.append(remote(ref, ref, red_s.at[sem], red_r.at[sem], device(axis, step)))
        return copies

    def copy4(part):
        return spread_copies(part, 1, rows_own(part), 30)

    def copy5(part):
        return spread_copies(part, 0, rows_at(part, 0), 39)

    def copy6(part, step):
        ref = total.at[rows_at(part, step), cols_of(part)]
        return remote(ref, ref, red_s.at[48 + part * 4 + step], red_r.at[48], sibling)

    def start(copies):
        for copy in copies:
            copy.start()

    def wait(copies):
        for copy in copies:
            copy.wait_recv()

    def reduce_step(level, part):
        if level == 0:
            wait(copy0(part))

            def some(i, carry):
                rows = pl.ds(pl.multiple_of(i * 64, 64), 64)
                value = keep[part, rows, :] + recv0[part, rows, :].astype(jnp.float32)
                keep[part, rows, :] = value
                send1[part, rows, :] = value.astype(jnp.bfloat16)
                return carry

            lax.fori_loop(0, 8, some, 0)
            start(copy1(part))
        elif level == 1:
            wait(copy1(part))
            own = pl.ds(pl.multiple_of(pos[order(part, 0)] * 128, 128), 128)
            value = keep[part, own, :]
            for step in range(3):
                value = value + recv1[part, step].astype(jnp.float32)
            keep1[part] = value
            send2[part] = value.astype(jnp.bfloat16)
            start(copy2(part))
        elif level == 2:
            wait(copy2(part))
            own = pl.ds(pl.multiple_of(pos[order(part, 1)] * 32, 32), 32)
            value = keep1[part, own, :]
            for step in range(3):
                value = value + recv2[part, step].astype(jnp.float32)
            recv3[part, pos[order(part, 2)]] = value.astype(jnp.bfloat16)
            start(copy3(part))
        elif level == 3:
            wait(copy3(part))
            value = recv3[part, 0].astype(jnp.float32)
            for step in range(1, 4):
                value = value + recv3[part, step].astype(jnp.float32)
            total[rows_own(part), cols_of(part)] = value.astype(jnp.bfloat16)
            start(copy4(part))
        elif level == 4:
            wait(copy4(part))
            start(copy5(part))
            copy6(part, 0).start()
        elif level == 5:
            for step, copy in zip((1, 3, 2), copy5(part)):
                copy.wait_recv()
                copy6(part, 4 - step).start()

    feat_grad[...] = jnp.zeros_like(feat_grad)
    cell_row = lax.broadcasted_iota(jnp.int32, (256, ROIS), 0)

    def reduce_at(k, slot):
        for level, due_slot in enumerate(SLOTS):
            if due_slot % 2 == slot:

                @pl.when(k == due_slot // 2)
                def _():
                    for part in range(3):
                        reduce_step(level, part)

    def backward(k, carry):
        for j in range(POOL):
            first = pl.multiple_of(k * SPAN + 256 * j, 256)
            dxs[256 * j : 256 * j + 256, :] = dot_nt(dpre1[...], weight(first, 256)).astype(jnp.bfloat16)
        reduce_at(k, 0)
        for q in range(4):
            for j in range(POOL):
                cells = cells_t[pl.ds(k * POOL + j, 1), :] - 256 * q
                hot = jnp.where(cell_row == cells, 1.0, 0.0).astype(jnp.bfloat16)
                xg[q, :, 256 * j : 256 * j + 256] = hot
            feat_grad[256 * q : 256 * q + 256, :] += dot(xg[q], dxs[...])
        reduce_at(k, 1)
        return carry

    lax.fori_loop(0, POOL, backward, 0)
    stores[1].start()
    for part in range(3):
        reduce_step(5, part)
    half_rows = total.at[pl.ds(theirs, 512)]
    pltpu.make_async_copy(half_rows, half_rows, red_r.at[48]).wait()
    stores[2].start()
    for part in range(3):
        for make in (copy0, copy1, copy2, copy3, copy4, copy5):
            for copy in make(part):
                copy.wait_send()
        for step in range(4):
            copy6(part, step).wait_send()
    for store in stores:
        store.wait()


PIECES = 4


def finish(neck_in, grad_in, total_in, neck, feat_grad, second_grad, out_grad, total, wide, turned, cells, grads, loaded, stored):
    rows = HID // PIECES
    copies = []
    for i in range(PIECES):
        part = pl.ds(i * rows, rows)
        for n, (src, held, dst) in enumerate(
            [(total_in, total, None), (grad_in, grads, feat_grad), (neck_in, cells, neck)]
        ):
            load = pltpu.make_async_copy(src.at[part], held.at[part], loaded.at[n, i])
            load.start()
            if dst is not None:
                copies.append((load, pltpu.make_async_copy(held.at[part], dst.at[part], stored.at[n, i])))
            else:
                wide_part = pltpu.make_async_copy(wide.at[part], second_grad.at[part], stored.at[0, i])
                copies.append((load, wide_part))
    last = pltpu.make_async_copy(turned, out_grad, stored.at[0, PIECES])
    for i in range(PIECES):
        part = slice(i * rows, (i + 1) * rows)
        for n in range(3):
            load, store = copies[3 * i + n]
            load.wait()
            if n == 0:
                wide[part, :] = total[part, 0:HID].astype(jnp.float32)
                turned[:, part] = total[part, HID:].astype(jnp.float32).T[0:OUTS]
            store.start()
    last.start()
    for load, store in copies:
        store.wait()
    last.wait()


def on_device(
    features,
    conv_weight,
    first_weight,
    second_weight,
    out_weight,
    roi_count,
    roi_row,
    roi_col,
    roi_angle,
    roi_label,
    roi_target,
):
    f32, bf16 = jnp.float32, jnp.bfloat16
    shift_rows, shift_cols = offset_tables(POOL, ANGLES)
    shift = (shift_rows * 32 + shift_cols).astype(np.float32)
    table = np.zeros((128, 128), np.float32)
    table[:ANGLES, :SAMPLES] = shift
    table_t = np.ascontiguousarray(table.T[:64])

    vmem = pl.BlockSpec(memory_space=pltpu.VMEM)
    hbm = pl.BlockSpec(memory_space=pl.ANY)
    smem = pl.BlockSpec(memory_space=pltpu.SMEM)
    dma = pltpu.SemaphoreType.DMA
    neck, feat_grad, total = pl.pallas_call(
        kernel,
        out_shape=(
            jax.ShapeDtypeStruct((CELLS, CH), bf16),
            jax.ShapeDtypeStruct((CELLS, CH), f32),
            jax.ShapeDtypeStruct((HID, WIDE), bf16),
        ),
        in_specs=[vmem, hbm, vmem, hbm, vmem, smem] + [vmem] * 7,
        out_specs=(hbm, hbm, hbm),
        scratch_shapes=[
            pltpu.VMEM((CELLS, CH), bf16),
            pltpu.VMEM((CELLS, CH), f32),
            pltpu.VMEM((HID, WIDE), bf16),
            pltpu.VMEM((2, 4, 4, 2, 2, GROUP, 128), bf16),
            pltpu.VMEM((3, 3 * CH, CH), bf16),
            pltpu.VMEM((HID, HID), bf16),
            pltpu.VMEM((128, HID), bf16),
            pltpu.VMEM((128, ROIS), f32),
            pltpu.VMEM((ROIS, 128), f32),
            pltpu.VMEM((2, 32, CH), f32),
            pltpu.VMEM((2, 32, CH), bf16),
            pltpu.VMEM((8, 112, 128), bf16),
            pltpu.VMEM((8, 112, 128), bf16),
            pltpu.VMEM((2, 32, CH), bf16),
            pltpu.VMEM((2, 32, CH), bf16),
            pltpu.VMEM((2, 2, 16, CH), bf16),
            pltpu.VMEM((2, 48, CH), f32),
            pltpu.VMEM((34, 32, CH), bf16),
            pltpu.VMEM((34, 32, 3 * CH), bf16),
            pltpu.VMEM((8, ROIS, SPAN), bf16),
            pltpu.VMEM((ROIS, CH), bf16),
            pltpu.VMEM((ROIS, 1024), f32),
            pltpu.VMEM((ROIS, 128), f32),
            pltpu.VMEM((64, ROIS), jnp.int32),
            pltpu.VMEM((ROIS, HID), f32),
            pltpu.VMEM((ROIS, HID), f32),
            pltpu.VMEM((ROIS, HID), f32),
            pltpu.VMEM((ROIS, HID), bf16),
            pltpu.VMEM((ROIS, HID), bf16),
            pltpu.VMEM((ROIS, HID), bf16),
            pltpu.VMEM((SPAN, CH), bf16),
            pltpu.VMEM((3, 512, COLS), f32),
            pltpu.VMEM((3, 512, COLS), bf16),
            pltpu.VMEM((3, 512, COLS), bf16),
            pltpu.VMEM((3, 512, COLS), bf16),
            pltpu.VMEM((3, 3, 128, COLS), bf16),
            pltpu.VMEM((3, 128, COLS), f32),
            pltpu.VMEM((3, 128, COLS), bf16),
            pltpu.VMEM((3, 3, 32, COLS), bf16),
            pltpu.VMEM((3, 4, 32, COLS), bf16),
            dma((8,)),
            dma((8,)),
            dma((7,)),
            dma((7,)),
            dma((108,)),
            dma((108,)),
            dma((48,)),
            dma((12,)),
            dma((60,)),
            dma((49,)),
            dma((2,)),
            dma((3,)),
        ],
        compiler_params=pltpu.CompilerParams(
            collective_id=0, has_side_effects=True, vmem_limit_bytes=60 * 2**20
        ),
    )(
        features,
        conv_weight.reshape(3, 3 * CH, CH),
        first_weight,
        second_weight,
        out_weight.T,
        roi_count,
        roi_row,
        roi_col,
        roi_angle,
        roi_label,
        roi_target.T,
        jnp.asarray(table, bf16),
        jnp.asarray(table_t, bf16),
    )
    neck, feat_grad, second_grad, out_grad = pl.pallas_call(
        finish,
        out_shape=(
            jax.ShapeDtypeStruct((CELLS, CH), bf16),
            jax.ShapeDtypeStruct((CELLS, CH), f32),
            jax.ShapeDtypeStruct((HID, HID), f32),
            jax.ShapeDtypeStruct((OUTS, HID), f32),
        ),
        in_specs=[hbm] * 3,
        out_specs=(hbm,) * 4,
        scratch_shapes=[
            pltpu.VMEM((HID, WIDE), bf16),
            pltpu.VMEM((HID, HID), f32),
            pltpu.VMEM((OUTS, HID), f32),
            pltpu.VMEM((CELLS, CH), bf16),
            pltpu.VMEM((CELLS, CH), f32),
            dma((3, PIECES)),
            dma((3, PIECES + 1)),
        ],
        compiler_params=pltpu.CompilerParams(vmem_limit_bytes=60 * 2**20),
    )(neck, feat_grad, total)
    return (
        neck.reshape(32, 32, CH),
        feat_grad.reshape(32, 32, CH),
        second_grad,
        out_grad.T,
    )


def solution(mesh):
    in_specs = (
        P("row", "col", None),
        P(),
        P(("row", "col"), None),
        P(),
        P(),
        P(("row", "col")),
        P(("row", "col")),
        P(("row", "col")),
        P(("row", "col")),
        P(("row", "col")),
        P(("row", "col"), None),
    )
    out_specs = (P("row", "col", None), P("row", "col", None), P(), P())
    return jax.shard_map(
        on_device, mesh=mesh, in_specs=in_specs, out_specs=out_specs, check_vma=False
    )
```

time: 144 us -> 117 us (0.81)
  Pallas kernels: 127 us -> 115 us
  other arithmetic: 8.54 us -> 0 us
  local copies, waits for them, and re-layouts: 6.95 us -> 0 us
    pallas_call x1, Pallas kernels: 127 us -> 111 us  [on_device(): pl.pallas_call(kernel, out_shape=(jax.ShapeDtypeStruct((CELLS, CH), bf16)...]
    convert_element_type x6 -> x0, other arithmetic: 7.25 us -> none  [the longest x1 4.19 us: on_device(): total[:, :HID].astype(f32)]
    pallas_call x0 -> x1, Pallas kernels: none -> 3.91 us  [on_device(): pl.pallas_call(finish, out_shape=(jax.ShapeDtypeStruct((CELLS, CH), bf16)...]
    unnamed x10 -> x0, local copies, waits for them, and re-layouts: 2.83 us -> none
where the time goes in v2:
time: 117 us
  Pallas kernels  115 us (98%)
  between operations  1.45 us (1%)
    pallas_call x1, Pallas kernels, on_device(): pl.pallas_call(kernel, out_shape=(jax.ShapeDtypeStruct((CELLS, CH), bf16)...  111 us
    pallas_call x1, Pallas kernels, on_device(): pl.pallas_call(finish, out_shape=(jax.ShapeDtypeStruct((CELLS, CH), bf16)...  3.91 us

profile of v2, /device:TPU:1, one launch (start us, length us, event | category | flops | bytes accessed | tf_op | source)
XLA Modules:
  0.0 116.5 jit_solution(16103369124686760101)
XLA Ops:
  1.3 111.2 %shard_map.156 = (bf16[1024,256]{1,0:T(8,128)(2,1)}, f32[1024,256]{1,0:T(8,128)}, bf16[1024,1152]{1,0:T(8,128)(2,1)}) custom-call(bf16[32,32,256]{2,1,0:T(8,128)(2,1)} %feat.1, bf16[3,768,256]{2,1,0:T(8,128)(2,1)} %bitcast.6, bf16[98,1024]{1,0:T(8,128)(2,1)} %shard.1, bf16[1024,1024]{1,0:T(8,128)(2,1)} %w2_hbm.1, bf16[42,1024]{1,0:T(8,128)(2,1)} %bitcast.7, ...), custom_call_target="tpu_custom_call" | custom-call | tf_op jit(solution)/shard_map/pallas_call | solution.py:835
  112.5 3.9 %shard_map.157 = (bf16[1024,256]{1,0:T(8,128)(2,1)}, f32[1024,256]{1,0:T(8,128)}, f32[1024,1024]{1,0:T(8,128)}, f32[42,1024]{1,0:T(8,128)}) custom-call(bf16[1024,256]{1,0:T(8,128)(2,1)} %get-tuple-element.11.neck_in, f32[1024,256]{1,0:T(8,128)} %get-tuple-element.12.grad_in, bf16[1024,1152]{1,0:T(8,128)(2,1)} %get-tuple-element.13.total_in), custom_call_target="tpu_custom_call" | custom-call | tf_op jit(solution)/shard_map/pallas_call | solution.py:916

commit v3 on v2

--- a/solution.py
+++ b/solution.py
@@ -23,7 +23,7 @@
 WIDE = HID + 128
 COLS = WIDE // 3
 MESH = pl.DeviceIdType.MESH
-SLOTS = (0, 5, 7, 9, 11)
+SLOTS = (3, 5, 7, 9, 12)
 
 prior_logit = -4.59512
 
@@ -235,7 +235,6 @@
     partners += [halo_device(a, b) for a, b in around]
     for partner in partners:
         pl.semaphore_signal(barrier, inc=1, device_id=partner, device_id_type=MESH)
-    pl.semaphore_wait(barrier, len(partners))
 
     def remote(src, dst, send_sem, recv_sem, target):
         return pltpu.make_async_remote_copy(
@@ -254,8 +253,10 @@
     stores = [
         pltpu.make_async_copy(neck, neck_hbm, out_s.at[0]),
         pltpu.make_async_copy(feat_grad, grad_hbm, out_s.at[1]),
-        pltpu.make_async_copy(total, total_hbm, out_s.at[2]),
     ]
+    for i, first in enumerate((core * 512, 512 - core * 512)):
+        rows = pl.ds(pl.multiple_of(first, 512), 512)
+        stores.append(pltpu.make_async_copy(total.at[rows], total_hbm.at[rows], out_s.at[2 + i]))
     for load in loads:
         load.start()
 
@@ -267,15 +268,34 @@
 
     for m in range(8):
         stage[m, 0:98, :] = shard[:, 128 * m : 128 * m + 128]
-    group_copies = [group_copy(step) for step in range(1, 8)]
-    for copy in group_copies:
-        copy.start()
-
     for i in range(32):
         cells_in_row = feat[i].astype(jnp.float32)
         edges[0, i : i + 1, :] = cells_in_row[0:1]
         edges[1, i : i + 1, :] = cells_in_row[31:32]
     edge_cols[...] = edges[...].astype(jnp.bfloat16)
+
+    facts[...] = jnp.zeros_like(facts)
+    position = lax.broadcasted_iota(jnp.int32, (1, ROIS), 1)
+    angle_row = roi_angle[...].reshape(1, ROIS)
+    base_row = roi_row[...].reshape(1, ROIS) * 32 + roi_col[...].reshape(1, ROIS)
+    facts[0:1, :] = base_row.astype(jnp.float32)
+    facts[1:2, :] = angle_row.astype(jnp.float32)
+    facts[2:3, :] = roi_label[...].reshape(1, ROIS).astype(jnp.float32)
+    facts[3:4, :] = jnp.where(position < count[0], 1.0, 0.0)
+    facts[CLASSES:OUTS, :] = roi_target[...].astype(jnp.float32)
+    meta[...] = facts[...].T
+    wo[...] = jnp.zeros_like(wo)
+    wo[0:OUTS, :] = out_w[...]
+    lane = lax.broadcasted_iota(jnp.int32, (ROIS, 128), 1)
+    angle_hot = jnp.where(lane == meta[:, 1:2].astype(jnp.int32), 1.0, 0.0).astype(jnp.bfloat16)
+    cells_all[...] = dot(angle_hot, table[...]) + meta[:, 0:1]
+    hot_t = jnp.where(lax.broadcasted_iota(jnp.int32, (128, ROIS), 0) == angle_row, 1.0, 0.0)
+    cells_t[...] = dot(table_t[...], hot_t.astype(jnp.bfloat16)).astype(jnp.int32) + base_row
+
+    pl.semaphore_wait(barrier, len(partners))
+    group_copies = [group_copy(step) for step in range(1, 8)]
+    for copy in group_copies:
+        copy.start()
 
     def halo_copy(index):
         a, b = around[index]
@@ -354,24 +374,6 @@
             line_copy(part, key, -1 if way == 0 else 1).start()
         if phase == 2 and half == 1 and (part, 2, key, 1, 1 - way) in got:
             line_copy(part, key, 2).start()
-
-    facts[...] = jnp.zeros_like(facts)
-    position = lax.broadcasted_iota(jnp.int32, (1, ROIS), 1)
-    angle_row = roi_angle[...].reshape(1, ROIS)
-    base_row = roi_row[...].reshape(1, ROIS) * 32 + roi_col[...].reshape(1, ROIS)
-    facts[0:1, :] = base_row.astype(jnp.float32)
-    facts[1:2, :] = angle_row.astype(jnp.float32)
-    facts[2:3, :] = roi_label[...].reshape(1, ROIS).astype(jnp.float32)
-    facts[3:4, :] = jnp.where(position < count[0], 1.0, 0.0)
-    facts[CLASSES:OUTS, :] = roi_target[...].astype(jnp.float32)
-    meta[...] = facts[...].T
-    wo[...] = jnp.zeros_like(wo)
-    wo[0:OUTS, :] = out_w[...]
-    lane = lax.broadcasted_iota(jnp.int32, (ROIS, 128), 1)
-    angle_hot = jnp.where(lane == meta[:, 1:2].astype(jnp.int32), 1.0, 0.0).astype(jnp.bfloat16)
-    cells_all[...] = dot(angle_hot, table[...]) + meta[:, 0:1]
-    hot_t = jnp.where(lax.broadcasted_iota(jnp.int32, (128, ROIS), 0) == angle_row, 1.0, 0.0)
-    cells_t[...] = dot(table_t[...], hot_t.astype(jnp.bfloat16)).astype(jnp.int32) + base_row
 
     slots[member] = stage[member]
     for copy in group_copies:
@@ -617,10 +619,6 @@
         keep[part] = half_grad(mine, slice(COLS * part, COLS * part + COLS))
     activate(pre1, None, gp1)
 
-    for n in range(4):
-        cols = slice(256 * n, 256 * n + 256)
-        dpre1[:, cols] = (dot_nt(dpre2[...], w2[cols, :]) * gp1[:, cols]).astype(jnp.bfloat16)
-
     def order(part, level):
         return PARTS[part][3][level]
 
@@ -630,7 +628,7 @@
     def scatter_copies(part, level, src, dst, rows, sems):
         copies = []
         axis = order(part, level)
-        for step in (1, 3, 2):
+        for step in (2, 1, 3):
             piece = src.at[part, pl.ds(pl.multiple_of(spot(axis, step) * rows, rows), rows)]
             sem = sems + part * 3 + step - 1
             copies.append(remote(piece, dst.at[part, step - 1], red_s.at[sem], red_r.at[sem], device(axis, step)))
@@ -645,7 +643,7 @@
     def copy3(part):
         copies = []
         axis = order(part, 2)
-        for step in (1, 3, 2):
+        for step in (2, 1, 3):
             sem = 21 + part * 3 + step - 1
             ref = recv3.at[part, pos[axis]]
             copies.append(remote(ref, ref, red_s.at[sem], red_r.at[sem], device(axis, step)))
@@ -661,7 +659,7 @@
     def spread_copies(part, level, rows, sems):
         copies = []
         axis = order(part, level)
-        for step in (1, 3, 2):
+        for step in (2, 1, 3):
             sem = sems + part * 3 + step - 1
             ref = total.at[rows, cols_of(part)]
             copies.append(remote(ref, ref, red_s.at[sem], red_r.at[sem], device(axis, step)))
@@ -689,15 +687,21 @@
         if level == 0:
             wait(copy0(part))
 
-            def some(i, carry):
-                rows = pl.ds(pl.multiple_of(i * 64, 64), 64)
-                value = keep[part, rows, :] + recv0[part, rows, :].astype(jnp.float32)
-                keep[part, rows, :] = value
-                send1[part, rows, :] = value.astype(jnp.bfloat16)
-                return carry
-
-            lax.fori_loop(0, 8, some, 0)
-            start(copy1(part))
+            for step, copy in zip((2, 1, 3, 0), copy1(part) + [None]):
+
+                def some(i, carry):
+                    first = spot(order(part, 0), step) * 128 + i * 64
+                    rows = pl.ds(pl.multiple_of(first, 64), 64)
+                    value = keep[part, rows, :] + recv0[part, rows, :].astype(jnp.float32)
+                    if step:
+                        send1[part, rows, :] = value.astype(jnp.bfloat16)
+                    else:
+                        keep[part, rows, :] = value
+                    return carry
+
+                lax.fori_loop(0, 2, some, 0)
+                if copy is not None:
+                    copy.start()
         elif level == 1:
             wait(copy1(part))
             own = pl.ds(pl.multiple_of(pos[order(part, 0)] * 128, 128), 128)
@@ -727,15 +731,22 @@
             start(copy5(part))
             copy6(part, 0).start()
         elif level == 5:
-            for step, copy in zip((1, 3, 2), copy5(part)):
+            for step, copy in zip((2, 1, 3), copy5(part)):
                 copy.wait_recv()
                 copy6(part, 4 - step).start()
 
+    for part in range(3):
+        reduce_step(0, part)
+
+    for n in range(4):
+        cols = slice(256 * n, 256 * n + 256)
+        dpre1[:, cols] = (dot_nt(dpre2[...], w2[cols, :]) * gp1[:, cols]).astype(jnp.bfloat16)
+
     feat_grad[...] = jnp.zeros_like(feat_grad)
     cell_row = lax.broadcasted_iota(jnp.int32, (256, ROIS), 0)
 
     def reduce_at(k, slot):
-        for level, due_slot in enumerate(SLOTS):
+        for level, due_slot in enumerate(SLOTS, 1):
             if due_slot % 2 == slot:
 
                 @pl.when(k == due_slot // 2)
@@ -759,11 +770,10 @@
 
     lax.fori_loop(0, POOL, backward, 0)
     stores[1].start()
-    for part in range(3):
-        reduce_step(5, part)
+    stores[2].start()
     half_rows = total.at[pl.ds(theirs, 512)]
     pltpu.make_async_copy(half_rows, half_rows, red_r.at[48]).wait()
-    stores[2].start()
+    stores[3].start()
     for part in range(3):
         for make in (copy0, copy1, copy2, copy3, copy4, copy5):
             for copy in make(part):
@@ -893,7 +903,7 @@
             dma((60,)),
             dma((49,)),
             dma((2,)),
-            dma((3,)),
+            dma((4,)),
         ],
         compiler_params=pltpu.CompilerParams(
             collective_id=0, has_side_effects=True, vmem_limit_bytes=60 * 2**20

time: 117 us -> 113 us (0.966)
  Pallas kernels: 115 us -> 112 us
    pallas_call x1, Pallas kernels: 111 us -> 108 us  [on_device(): pl.pallas_call(kernel, out_shape=(jax.ShapeDtypeStruct((CELLS, CH), bf16)...]
where the time goes in v3:
time: 113 us
  Pallas kernels  112 us (99%)
  between operations  1.45 us (1%)
    pallas_call x1, Pallas kernels, on_device(): pl.pallas_call(kernel, out_shape=(jax.ShapeDtypeStruct((CELLS, CH), bf16)...  108 us
    pallas_call x1, Pallas kernels, on_device(): pl.pallas_call(finish, out_shape=(jax.ShapeDtypeStruct((CELLS, CH), bf16)...  3.91 us

profile of v3, /device:TPU:1, one launch (start us, length us, event | category | flops | bytes accessed | tf_op | source)
XLA Modules:
  0.0 113.3 jit_solution(15944205890172006006)
XLA Ops:
  1.3 108.0 %shard_map.156 = (bf16[1024,256]{1,0:T(8,128)(2,1)}, f32[1024,256]{1,0:T(8,128)}, bf16[1024,1152]{1,0:T(8,128)(2,1)}) custom-call(bf16[32,32,256]{2,1,0:T(8,128)(2,1)} %feat.1, bf16[3,768,256]{2,1,0:T(8,128)(2,1)} %bitcast.6, bf16[98,1024]{1,0:T(8,128)(2,1)} %shard.1, bf16[1024,1024]{1,0:T(8,128)(2,1)} %w2_hbm.1, bf16[42,1024]{1,0:T(8,128)(2,1)} %bitcast.7, ...), custom_call_target="tpu_custom_call" | custom-call | tf_op jit(solution)/shard_map/pallas_call | solution.py:845
  109.3 3.9 %shard_map.157 = (bf16[1024,256]{1,0:T(8,128)(2,1)}, f32[1024,256]{1,0:T(8,128)}, f32[1024,1024]{1,0:T(8,128)}, f32[42,1024]{1,0:T(8,128)}) custom-call(bf16[1024,256]{1,0:T(8,128)(2,1)} %get-tuple-element.11.neck_in, f32[1024,256]{1,0:T(8,128)} %get-tuple-element.12.grad_in, bf16[1024,1152]{1,0:T(8,128)(2,1)} %get-tuple-element.13.total_in), custom_call_target="tpu_custom_call" | custom-call | tf_op jit(solution)/shard_map/pallas_call | solution.py:926

commit v4 on v3

--- a/solution.py
+++ b/solution.py
@@ -453,56 +453,49 @@
     def entries(z, c, high, first):
         return xg[z * 2 + c, :, pl.ds(pl.multiple_of(768 * high + first, 256), 256)]
 
-    def product(part, far):
+    def product(part, far, i):
         axis = PARTS[part][3][2]
         here = spot(axis, far)
-        line_wait(part, far)
+        if i == 0:
+            line_wait(part, far)
         if axis == "z":
             pairs = [(c, high) for c in range(2) for high in range(2)]
             left = jnp.concatenate([entries(here, c, high, 0) for c, high in pairs], axis=1)
-            for n in range(4):
-                low, y = n // 2, 2 * (n % 2)
-                halves = [
-                    jnp.concatenate([wf[low, y + i, here, c, high, 0:256, :] for c, high in pairs], axis=0)
-                    for i in range(2)
-                ]
-                pre1[:, 256 * n : 256 * n + 256] += dot(left, jnp.concatenate(halves, axis=1))
+            low, y = i // 2, 2 * (i % 2)
+            halves = [
+                jnp.concatenate([wf[low, y + n, here, c, high, 0:256, :] for c, high in pairs], axis=0)
+                for n in range(2)
+            ]
+            pre1[:, 256 * i : 256 * i + 256] += dot(left, jnp.concatenate(halves, axis=1))
         elif axis == "x":
             low, high = lax.rem(here, 2), here // 2
-            for z in range(0, 4, 2):
-                pairs = [(z + i, c) for i in range(2) for c in range(2)]
-                left = jnp.concatenate([entries(a, c, high, 256) for a, c in pairs], axis=1)
-                for n in range(2):
-                    halves = [
-                        jnp.concatenate([wf[low, 2 * n + i, a, c, high, 256:512, :] for a, c in pairs], axis=0)
-                        for i in range(2)
-                    ]
-                    cols = pl.ds(pl.multiple_of(512 * low + 256 * n, 256), 256)
-                    pre1[:, cols] += dot(left, jnp.concatenate(halves, axis=1))
+            z, n = 2 * (i // 2), i % 2
+            pairs = [(z + a, c) for a in range(2) for c in range(2)]
+            left = jnp.concatenate([entries(a, c, high, 256) for a, c in pairs], axis=1)
+            halves = [
+                jnp.concatenate([wf[low, 2 * n + b, a, c, high, 256:512, :] for a, c in pairs], axis=0)
+                for b in range(2)
+            ]
+            cols = pl.ds(pl.multiple_of(512 * low + 256 * n, 256), 256)
+            pre1[:, cols] += dot(left, jnp.concatenate(halves, axis=1))
         else:
-
-            def some(z, carry):
-                pairs = [(c, high) for c in range(2) for high in range(2)]
-                left = jnp.concatenate([entries(z, c, high, 512) for c, high in pairs], axis=1)
+            pairs = [(c, high) for c in range(2) for high in range(2)]
+            left = jnp.concatenate([entries(i, c, high, 512) for c, high in pairs], axis=1)
+            halves = [
+                jnp.concatenate([wf[low, here, i, c, high, 512:768, :] for c, high in pairs], axis=0)
+                for low in range(2)
+            ]
+            value = dot(left, jnp.concatenate(halves, axis=1))
+            if i == 3:
+                groups = [(z, c, high) for z in range(4) for c in range(2) for high in range(2)]
                 halves = [
-                    jnp.concatenate([wf[low, here, z, c, high, 512:768, :] for c, high in pairs], axis=0)
+                    jnp.concatenate([wf[low, here, z, c, high, 768:784, :] for z, c, high in groups], axis=0)
                     for low in range(2)
                 ]
-                add(dot(left, jnp.concatenate(halves, axis=1)))
-                return carry
-
-            def add(value):
-                for low in range(2):
-                    cols = pl.ds(pl.multiple_of(512 * low + 128 * here, 128), 128)
-                    pre1[:, cols] += value[:, 128 * low : 128 * low + 128]
-
-            lax.fori_loop(0, 4, some, 0)
-            groups = [(z, c, high) for z in range(4) for c in range(2) for high in range(2)]
-            halves = [
-                jnp.concatenate([wf[low, here, z, c, high, 768:784, :] for z, c, high in groups], axis=0)
-                for low in range(2)
-            ]
-            add(dot(xt[...], jnp.concatenate(halves, axis=1)))
+                value = value + dot(xt[...], jnp.concatenate(halves, axis=1))
+            for low in range(2):
+                cols = pl.ds(pl.multiple_of(512 * low + 128 * here, 128), 128)
+                pre1[:, cols] += value[:, 128 * low : 128 * low + 128]
 
     events = arrivals()
     now = 3.0
@@ -534,15 +527,15 @@
         part, phase, key, half, way = item
         far = 0 if phase < 2 else 2 if half else -1 if way == 0 else 1
         due[(part, far)] = max(due.get((part, far), 0.0), time + 3.0)
-    todo = sorted((time, key) for key, time in due.items())
+    todo = sorted((time, key + (i,)) for key, time in due.items() for i in range(4))
     while todo or events:
-        if events and (events[0][0] <= now + 0.3 or not todo):
+        if events and (events[0][0] <= now + 0.1 or not todo):
             time, item = events.pop(0)
             now = max(now + 0.05, time)
             arrive(item)
         elif todo and (todo[0][0] <= now or not events):
             product(*todo.pop(0)[1])
-            now += 0.7
+            now += 0.25
         else:
             now = min(events[0][0], todo[0][0])
     for copy in group_copies + halo_copies:

time: 113 us -> 111 us (0.982)
  Pallas kernels: 112 us -> 110 us
    pallas_call x1, Pallas kernels: 108 us -> 106 us  [on_device(): pl.pallas_call(kernel, out_shape=(jax.ShapeDtypeStruct((CELLS, CH), bf16)...]
where the time goes in v4:
time: 111 us
  Pallas kernels  110 us (99%)
  between operations  1.45 us (1%)
    pallas_call x1, Pallas kernels, on_device(): pl.pallas_call(kernel, out_shape=(jax.ShapeDtypeStruct((CELLS, CH), bf16)...  106 us
    pallas_call x1, Pallas kernels, on_device(): pl.pallas_call(finish, out_shape=(jax.ShapeDtypeStruct((CELLS, CH), bf16)...  3.91 us

profile of v4, /device:TPU:1, one launch (start us, length us, event | category | flops | bytes accessed | tf_op | source)
XLA Modules:
  0.0 111.0 jit_solution(2829849670346629768)
XLA Ops:
  1.3 105.6 %shard_map.156 = (bf16[1024,256]{1,0:T(8,128)(2,1)}, f32[1024,256]{1,0:T(8,128)}, bf16[1024,1152]{1,0:T(8,128)(2,1)}) custom-call(bf16[32,32,256]{2,1,0:T(8,128)(2,1)} %feat.1, bf16[3,768,256]{2,1,0:T(8,128)(2,1)} %bitcast.6, bf16[98,1024]{1,0:T(8,128)(2,1)} %shard.1, bf16[1024,1024]{1,0:T(8,128)(2,1)} %w2_hbm.1, bf16[42,1024]{1,0:T(8,128)(2,1)} %bitcast.7, ...), custom_call_target="tpu_custom_call" | custom-call | tf_op jit(solution)/shard_map/pallas_call | solution.py:838
  106.9 3.9 %shard_map.157 = (bf16[1024,256]{1,0:T(8,128)(2,1)}, f32[1024,256]{1,0:T(8,128)}, f32[1024,1024]{1,0:T(8,128)}, f32[42,1024]{1,0:T(8,128)}) custom-call(bf16[1024,256]{1,0:T(8,128)(2,1)} %get-tuple-element.11.neck_in, f32[1024,256]{1,0:T(8,128)} %get-tuple-element.12.grad_in, bf16[1024,1152]{1,0:T(8,128)(2,1)} %get-tuple-element.13.total_in), custom_call_target="tpu_custom_call" | custom-call | tf_op jit(solution)/shard_map/pallas_call | solution.py:919

commit v5 on v4

--- a/solution.py
+++ b/solution.py
@@ -502,7 +502,7 @@
     batches = []
     for g in range(16):
         batches.append([])
-        while events and events[0][0] <= now + 0.5:
+        while events and events[0][0] <= now + 1.0:
             time, item = events.pop(0)
             now = max(now + 0.05, time)
             batches[-1].append(item)

time: 111 us -> 110 us (level)
  Pallas kernels: 110 us -> 108 us
    pallas_call x1, Pallas kernels: 106 us -> 104 us  [on_device(): pl.pallas_call(kernel, out_shape=(jax.ShapeDtypeStruct((CELLS, CH), bf16)...]
where the time goes in v5:
time: 110 us
  Pallas kernels  108 us (98%)
  between operations  1.45 us (1%)
    pallas_call x1, Pallas kernels, on_device(): pl.pallas_call(kernel, out_shape=(jax.ShapeDtypeStruct((CELLS, CH), bf16)...  104 us
    pallas_call x1, Pallas kernels, on_device(): pl.pallas_call(finish, out_shape=(jax.ShapeDtypeStruct((CELLS, CH), bf16)...  3.91 us

profile of v5, /device:TPU:1, one launch (start us, length us, event | category | flops | bytes accessed | tf_op | source)
XLA Modules:
  0.0 109.8 jit_solution(709426311406873038)
XLA Ops:
  1.3 104.4 %shard_map.156 = (bf16[1024,256]{1,0:T(8,128)(2,1)}, f32[1024,256]{1,0:T(8,128)}, bf16[1024,1152]{1,0:T(8,128)(2,1)}) custom-call(bf16[32,32,256]{2,1,0:T(8,128)(2,1)} %feat.1, bf16[3,768,256]{2,1,0:T(8,128)(2,1)} %bitcast.6, bf16[98,1024]{1,0:T(8,128)(2,1)} %shard.1, bf16[1024,1024]{1,0:T(8,128)(2,1)} %w2_hbm.1, bf16[42,1024]{1,0:T(8,128)(2,1)} %bitcast.7, ...), custom_call_target="tpu_custom_call" | custom-call | tf_op jit(solution)/shard_map/pallas_call | solution.py:838
  105.7 3.9 %shard_map.157 = (bf16[1024,256]{1,0:T(8,128)(2,1)}, f32[1024,256]{1,0:T(8,128)}, f32[1024,1024]{1,0:T(8,128)}, f32[42,1024]{1,0:T(8,128)}) custom-call(bf16[1024,256]{1,0:T(8,128)(2,1)} %get-tuple-element.11.neck_in, f32[1024,256]{1,0:T(8,128)} %get-tuple-element.12.grad_in, bf16[1024,1152]{1,0:T(8,128)(2,1)} %get-tuple-element.13.total_in), custom_call_target="tpu_custom_call" | custom-call | tf_op jit(solution)/shard_map/pallas_call | solution.py:919
